TPU v7x, 256 devices: a whole 4x4x8 slice. The times are simulated.
256 devices in a mesh: dp: 64 (over y, z, core), tensor: 4 (over x).
Axes of the slice: x: 4, y: 4, z: 8, core: 2. Of those that a mesh axis runs over, the one named last changes fastest.
Arguments:
- patches: bfloat16 [32768, 1280], P('dp', 'tensor'), may hold values from -64 to 64
- counts: int32 [512], replicated, may hold values from 32 to 64, as said below
- source_slot: int32 [512], replicated, may hold values from 0 to 511, as said below
- target_slot: int32 [512], replicated, may hold values from 0 to 511, as said below
- lang_start: int32 [512], replicated, may hold values from 0 to 10232, as said below
- window_order: int32 [512, 16], replicated, may hold values from 0 to 15, as said below
- norm_gain: float32 [1280], replicated, may hold values from 0.1 to 1.9
- qkv_weight: bfloat16 [1280, 3, 1280], P(None, None, 'tensor'), may hold values from -1 to 1
- qkv_bias: float32 [3, 1280], P(None, 'tensor'), may hold values from -3 to 3
- proj_weight: bfloat16 [1280, 1280], P('tensor'), may hold values from -0.15625 to 0.15625
- proj_bias: float32 [1280], replicated, may hold values from -3 to 3
- merge_gain: float32 [1280], replicated, may hold values from 0.1 to 1.9
- expand_weight: bfloat16 [5120, 2560], P('dp', 'tensor'), may hold values from -0.078125 to 0.078125
- expand_bias: float32 [2560], P('tensor'), may hold values from -3 to 3
- output_weight: bfloat16 [2560, 4096], P('tensor', 'dp'), may hold values from -0.125 to 0.125
- output_bias: float32 [4096], P('tensor'), may hold values from -3 to 3
Outputs:
- encoded: bfloat16 [32768, 1280], P('dp', 'tensor')
- merged: bfloat16 [10240, 4096], P('dp', 'tensor')
Inputs may be any that keep to these rules, and one draw needn't show every extreme that they name: `counts`: each count is a multiple of 4. `source_slot`: A permutation of the 512 slots; slot s lies on data rank s // 8. `target_slot`: A permutation of the slots; at most 1 images go from one source rank to one target rank. `lang_start`: image i's merged rows lie inside the shard of rank i // 8 (160 rows each), in increasing order of i without intersection; at most 1 images go from one target rank to one shard. `window_order`: for image i the first counts[i] / 4 entries are a permutation of 0 to counts[i] / 4 - 1; entry j beyond them is j.
All inputs are finite; a program needn't handle non-finite values.
Results may differ from a plain program's by a relative error of at most 0.019.
Values may be sent and summed in bfloat16 or wider, within the bound.
No kernel may reach another device: no remote copies, remote signals or barrier semaphores. Data moves between devices by JAX's collectives and lax.ppermute only.
A program may use at most 64 MiB of HBM per device.

v0:
```python
import math

import jax
import jax.numpy as jnp
from jax import lax
from jax.sharding import PartitionSpec as P

HD = 80
LROWS = 160


EPSILON = 1e-06


def rms_rows(values, row_gain):
    values = values.astype(jnp.float32)
    mean_square = jnp.mean(values * values, axis=-1, keepdims=True)
    return values * lax.rsqrt(mean_square + EPSILON) * row_gain


def rank_within(group_ids, image_ids):
    same_group = group_ids[:, None] == group_ids[None, :]
    before = image_ids[None, :] < image_ids[:, None]
    return jnp.sum(jnp.logical_and(same_group, before), axis=1)


def place_rows(slot_index, payload, total_rows):
    picks = (jnp.arange(total_rows, dtype=jnp.int32)[:, None] == slot_index[None, :]).astype(
        payload.dtype
    )
    return jnp.dot(picks, payload, preferred_element_type=jnp.float32).astype(payload.dtype)


def take_rows(slot_index, payload):
    picks = (slot_index[:, None] == jnp.arange(payload.shape[0], dtype=jnp.int32)[None, :]).astype(
        payload.dtype
    )
    return jnp.dot(picks, payload, preferred_element_type=jnp.float32).astype(payload.dtype)


def inverse_of(slots):
    return (
        jnp.zeros(slots.shape, jnp.int32).at[slots].set(jnp.arange(slots.shape[0], dtype=jnp.int32))
    )


def per_device(
    patches,
    counts,
    source_slot,
    target_slot,
    lang_start,
    window_order,
    norm_gain,
    qkv_weight,
    qkv_bias,
    proj_weight,
    proj_bias,
    merge_gain,
    expand_weight,
    expand_bias,
    output_weight,
    output_bias,
):
    dp_ranks = lax.axis_size("dp")
    dp_index = lax.axis_index("dp")
    groups = lax.axis_size("tensor")
    member = lax.axis_index("tensor")
    per_rank = counts.shape[0] // dp_ranks
    cols_here = patches.shape[1]
    slot_rows = patches.shape[0] // per_rank
    pair_slots = (per_rank + dp_ranks - 1) // dp_ranks
    model_width = cols_here * groups
    heads_here = cols_here // HD
    merged_depth = slot_rows // 4
    slot_ids = jnp.arange(per_rank, dtype=jnp.int32)
    row_ids = jnp.arange(slot_rows, dtype=jnp.int32)
    held_images = lax.dynamic_slice_in_dim(inverse_of(source_slot), dp_index * per_rank, per_rank)
    bound_images = lax.dynamic_slice_in_dim(inverse_of(target_slot), dp_index * per_rank, per_rank)
    outward = target_slot[held_images] // per_rank
    send_index = outward * pair_slots + rank_within(outward, held_images)
    outgoing = place_rows(
        send_index, patches.reshape(per_rank, slot_rows * cols_here), dp_ranks * pair_slots
    )
    incoming = lax.all_to_all(outgoing, "dp", split_axis=0, concat_axis=0, tiled=True)
    inward = source_slot[bound_images] // per_rank
    recv_index = inward * pair_slots + rank_within(inward, bound_images)
    arrived = take_rows(recv_index, incoming)
    arrived = arrived.reshape(per_rank * slot_rows, cols_here)
    full_rows = lax.all_gather(arrived, "tensor", axis=1, tiled=True)
    live_count = counts[bound_images]
    live_grid = row_ids[None, :] < live_count[:, None]
    live_rows = live_grid.reshape(per_rank * slot_rows, 1)
    normed = rms_rows(full_rows, norm_gain).astype(jnp.bfloat16)
    qkv_rows = jnp.dot(
        normed, qkv_weight.reshape(model_width, 3 * cols_here), preferred_element_type=jnp.float32
    )
    qkv_rows = (qkv_rows + qkv_bias.reshape(3 * cols_here)).astype(jnp.bfloat16)
    qkv_rows = qkv_rows.reshape(per_rank, slot_rows, 3, heads_here, HD)
    scores = jnp.einsum(
        "bqhe,bkhe->bhqk", qkv_rows[:, :, 0], qkv_rows[:, :, 1], preferred_element_type=jnp.float32
    )
    scores = scores * (1.0 / math.sqrt(HD))
    scores = jnp.where(live_grid[:, None, None, :], scores, -1e30)
    weights = jax.nn.softmax(scores, axis=-1).astype(jnp.bfloat16)
    context = jnp.einsum(
        "bhqk,bkhe->bqhe", weights, qkv_rows[:, :, 2], preferred_element_type=jnp.float32
    )
    context = context.astype(jnp.bfloat16).reshape(per_rank * slot_rows, cols_here)
    partial_out = jnp.dot(context, proj_weight, preferred_element_type=jnp.float32)
    summed = lax.psum(partial_out.astype(jnp.bfloat16), "tensor").astype(jnp.float32)
    hidden = full_rows.astype(jnp.float32) + summed + proj_bias
    hidden = jnp.where(live_rows, hidden, 0.0).astype(jnp.bfloat16)
    encoded = lax.dynamic_slice_in_dim(hidden, member * cols_here, cols_here, 1)
    merge_in = rms_rows(hidden, merge_gain).astype(jnp.bfloat16)
    merge_in = merge_in.reshape(per_rank * merged_depth, 4 * model_width)
    expand_full, output_full = (
        lax.all_gather(expand_weight, "dp", axis=0, tiled=True),
        lax.all_gather(output_weight, "dp", axis=1, tiled=True),
    )
    expanded = jnp.dot(merge_in, expand_full, preferred_element_type=jnp.float32) + expand_bias
    expanded = jax.nn.gelu(expanded, approximate=False).astype(jnp.bfloat16)
    spread = jnp.dot(expanded, output_full, preferred_element_type=jnp.float32)
    merged_rows = (
        lax.psum_scatter(
            spread.astype(jnp.bfloat16), "tensor", scatter_dimension=1, tiled=True
        ).astype(jnp.float32)
        + output_bias
    ).astype(jnp.bfloat16)
    merged_cols = merged_rows.shape[1]
    order_rows = window_order[bound_images]
    picker = (
        order_rows[:, :, None] == jnp.arange(merged_depth, dtype=jnp.int32)[None, None, :]
    ).astype(jnp.bfloat16)
    reordered = jnp.einsum(
        "bjm,bmc->bjc",
        picker,
        merged_rows.reshape(per_rank, merged_depth, merged_cols),
        preferred_element_type=jnp.float32,
    )
    reordered = reordered.astype(jnp.bfloat16)
    toward = bound_images // per_rank
    lang_index = toward * pair_slots + rank_within(toward, bound_images)
    leaving = place_rows(
        lang_index, reordered.reshape(per_rank, merged_depth * merged_cols), dp_ranks * pair_slots
    )
    landed = lax.all_to_all(leaving, "dp", split_axis=0, concat_axis=0, tiled=True)
    own_images = dp_index * per_rank + slot_ids
    anchor = target_slot[own_images] // per_rank
    land_index = anchor * pair_slots + rank_within(anchor, own_images)
    pieces = take_rows(land_index, landed)
    pieces = pieces.reshape(per_rank * merged_depth, merged_cols)
    first_row = lang_start[own_images] - dp_index * LROWS
    used_rows = counts[own_images] // 4
    step_ids = jnp.arange(merged_depth, dtype=jnp.int32)
    target = jnp.where(
        step_ids[None, :] < used_rows[:, None], first_row[:, None] + step_ids[None, :], LROWS
    )
    merged = (
        jnp.zeros((LROWS, merged_cols), jnp.bfloat16)
        .at[target.reshape(-1)]
        .set(pieces, mode="drop")
    )
    return (encoded, merged)


def solution(mesh):
    in_specs = (
        P("dp", "tensor"),
        P(),
        P(),
        P(),
        P(),
        P(),
        P(),
        P(None, None, "tensor"),
        P(None, "tensor"),
        P("tensor", None),
        P(),
        P(),
        P("dp", "tensor"),
        P("tensor"),
        P("tensor", "dp"),
        P("tensor"),
    )
    out_specs = (P("dp", "tensor"), P("dp", "tensor"))
    return jax.shard_map(
        per_device, mesh=mesh, in_specs=in_specs, out_specs=out_specs, check_vma=False
    )
```

profile of v0, /device:TPU:1, one launch (start us, length us, event | category | flops | bytes accessed | tf_op | source)
XLA Modules:
  0.0 463.2 jit_solution(6094012921511935232)
XLA Ops:
  8.0 1.3 copy.59
  11.1 2.4 scatter_custom_fusion.1
  13.6 2.4 scatter_custom_fusion
  16.1 1.3 gather_fusion.2
  17.7 2.4 fusion.1
  20.5 5.1 %reduce = bf16[64,20480]{1,0:T(8,128)(2,1)} reduce(bf16[64,1,20480]{2,0,1:T(8,128)(2,1)} %fusion.1, bf16[]{:T(256)} %broadcast.467), dimensions={1}, to_apply=%copy.60.reduce_sub_computation | reduce | bytes 5242882 | tf_op jit(solution)/shard_map/all_to_all | solution.py:85
  25.6 4.9 %reshape.414 = bf16[64,2,10240]{2,1,0:T(2,128)(2,1)} reshape(bf16[64,20480]{1,0:T(8,128)(2,1)} %reduce) | data formatting | bytes 5242880
  30.5 13.5 %all-to-all-start = ((bf16[64,2,10240]{2,1,0:T(2,128)(2,1)}), bf16[64,2,10240]{2,1,0:T(2,128)(2,1)}, u32[]{:S(2)}, u32[]{:S(2)}) async-start(bf16[64,2,10240]{2,1,0:T(2,128)(2,1)} %reshape.414), calls=%async_computation | async-start | bytes 5242880 | tf_op jit(solution)/shard_map/all_to_all | solution.py:85
  44.9 61.3 %all-to-all-done = bf16[64,2,10240]{2,1,0:T(2,128)(2,1)} async-done(((bf16[64,2,10240]{2,1,0:T(2,128)(2,1)}), bf16[64,2,10240]{2,1,0:T(2,128)(2,1)}, u32[]{:S(2)}, u32[]{:S(2)}) %all-to-all-start) | async-done | bytes 2621472 | tf_op jit(solution)/shard_map/all_to_all | solution.py:85
  106.2 16.3 %reshape.415 = bf16[64,1,20480]{2,1,0:T(2,128)(2,1)} reshape(bf16[64,2,10240]{2,1,0:T(2,128)(2,1)} %all-to-all-done) | data formatting | bytes 5242880
  122.5 5.4 %convolution_convert_fusion.1 = bf16[8,20480]{1,0:T(8,128)(2,1)S(1)} fusion(bf16[64,1,20480]{2,1,0:T(2,128)(2,1)} %reshape.415, s32[8]{0:T(128)S(1)} %fusion.135), kind=kOutput, calls=%fused_computation.13 | convolution fusion | flops 21135872 | bytes 2949152 | tf_op jit(solution)/shard_map/dot_general | solution.py:38
  130.3 21.9 %all-gather.4.cloned.1.call-done = bf16[512,1280]{0,1:T(8,128)(2,1)} async-done(((bf16[512,320]{0,1:T(8,128)(2,1)}), bf16[512,1280]{0,1:T(8,128)(2,1)}) %all-gather.4.cloned.1.call-update) | async-done | bytes 1310736 | tf_op jit(solution)/shard_map/all_gather | solution.py:90
  152.1 2.4 copy.62
  154.6 1.6 fusion.6
  156.3 2.9 add_convert_fusion
  161.3 1.5 copy.79
  162.9 1.5 copy.78
  167.2 1.9 convolution_convert_fusion.5
  170.4 52.4 %all-reduce.2.cloned.1.call-done = bf16[512,1280]{1,0:T(8,128)(2,1)} async-done(((bf16[512,1280]{1,0:T(8,128)(2,1)}), bf16[512,1280]{1,0:T(8,128)(2,1)}) %all-reduce.2.cloned.1.call-update) | async-done | bytes 1310736 | tf_op jit(solution)/shard_map/psum | solution.py:111
  222.8 2.2 fusion.3
  226.4 1.7 reshape.317
  228.1 26.7 %all-gather.8.cloned.1.call-done = bf16[640,4096]{0,1:T(8,128)(2,1)} async-done(((bf16[640,64]{0,1:T(8,128)(2,1)}), bf16[640,4096]{0,1:T(8,128)(2,1)}) %all-gather.8.cloned.1.call-update) | async-done | bytes 5242896 | tf_op jit(solution)/shard_map/all_gather | solution.py:119
  254.8 80.8 %all-gather.6.cloned.1.call-done = bf16[5120,640]{1,0:T(8,128)(2,1)} async-done(((bf16[80,640]{1,0:T(8,128)(2,1)}), bf16[5120,640]{1,0:T(8,128)(2,1)}) %all-gather.6.cloned.1.call-update) | async-done | bytes 6553616 | tf_op jit(solution)/shard_map/all_gather | solution.py:118
  335.6 9.1 %convolution_convert_fusion.4 = bf16[128,4096]{1,0:T(8,128)(2,1)} fusion(bf16[640,4096]{0,1:T(8,128)(2,1)} %all-gather.8.cloned.1.call-done, bf16[128,5120]{1,0:T(8,128)(2,1)} %reshape.317, bf16[5120,640]{1,0:T(8,128)(2,1)} %all-gather.6.cloned.1.call-done, f32[640]{0:T(1024)S(1)} %copy-done.15), kind=kOutput, calls=%fused_computation.17 | convolution fusion | flops 1515880448 | bytes 14158336 | tf_op jit(solution)/shard_map/dot_general | solution.py:123
  345.5 20.5 %reduce-scatter.2.cloned.1.call-done = bf16[128,1024]{1,0:T(8,128)(2,1)} async-done(((bf16[128,4096]{1,0:T(8,128)(2,1)}), bf16[128,1024]{1,0:T(8,128)(2,1)}) %reduce-scatter.2.cloned.1.call-update) | async-done | bytes 262160 | tf_op jit(solution)/shard_map/reduce_scatter | solution.py:125
  368.1 2.9 reduce.1
  371.0 4.5 reshape.416
  375.5 12.4 %all-to-all-start.1 = ((bf16[64,2,8192]{2,1,0:T(2,128)(2,1)}), bf16[64,2,8192]{2,1,0:T(2,128)(2,1)}, u32[]{:S(2)}, u32[]{:S(2)}) async-start(bf16[64,2,8192]{2,1,0:T(2,128)(2,1)} %reshape.416), calls=%async_computation.2 | async-start | bytes 4194304 | tf_op jit(solution)/shard_map/all_to_all | solution.py:147
  392.4 46.6 %all-to-all-done.1 = bf16[64,2,8192]{2,1,0:T(2,128)(2,1)} async-done(((bf16[64,2,8192]{2,1,0:T(2,128)(2,1)}), bf16[64,2,8192]{2,1,0:T(2,128)(2,1)}, u32[]{:S(2)}, u32[]{:S(2)}) %all-to-all-start.1) | async-done | bytes 2097184 | tf_op jit(solution)/shard_map/all_to_all | solution.py:147
  439.1 10.6 %reshape.417 = bf16[64,1,16384]{2,1,0:T(2,128)(2,1)} reshape(bf16[64,2,8192]{2,1,0:T(2,128)(2,1)} %all-to-all-done.1) | data formatting | bytes 4194304
  449.7 4.5 convolution_convert_fusion.3
  454.3 1.8 scatter_custom_fusion.2
  (99 shorter events, 21.0 us)
Async XLA Ops:
  8.0 148.2 %copy-start = (bf16[1280,3,320]{0,2,1:T(8,128)(2,1)S(1)}, bf16[1280,3,320]{0,2,1:T(8,128)(2,1)}, u32[]{:S(2)}) copy-start(bf16[1280,3,320]{0,2,1:T(8,128)(2,1)} %param.23) | copy-start | bytes 7372804
  30.5 13.5 %copy-start.4 = (s32[512]{0:T(512)S(1)}, s32[512]{0:T(512)}, u32[]{:S(2)}) copy-start(s32[512]{0:T(512)} %param.18) | copy-start | bytes 6148
  30.5 75.7 %all-to-all-start = ((bf16[64,2,10240]{2,1,0:T(2,128)(2,1)}), bf16[64,2,10240]{2,1,0:T(2,128)(2,1)}, u32[]{:S(2)}, u32[]{:S(2)}) async-start(bf16[64,2,10240]{2,1,0:T(2,128)(2,1)} %reshape.414), calls=%async_computation | async-start | bytes 5242880 | tf_op jit(solution)/shard_map/all_to_all | solution.py:85
  44.0 108.2 %all-gather.4.cloned.1.call-start = ((), (), s32[]{:S(2)}) async-start(), calls=%async_computation.3 | async-start | bytes 1638400 | tf_op jit(solution)/shard_map/all_gather | solution.py:90
  122.5 7.0 %copy-start.12 = (f32[3,320]{1,0:T(4,128)S(1)}, f32[3,320]{1,0:T(4,128)}, u32[]{:S(2)}) copy-start(f32[3,320]{1,0:T(4,128)} %param.24) | copy-start | bytes 11524
  122.5 7.1 %copy-start.3 = (s32[512]{0:T(512)S(1)}, s32[512]{0:T(512)}, u32[]{:S(2)}) copy-start(s32[512]{0:T(512)} %param.17) | copy-start | bytes 6148
  128.3 28.0 %copy-start.14 = (f32[1280]{0:T(1024)S(1)}, f32[1280]{0:T(1024)}, u32[]{:S(2)}) copy-start(f32[1280]{0:T(1024)} %param.22) | copy-start | bytes 15364
  129.2 93.5 %all-reduce.2.cloned.1.call-start = ((), (), s32[]{:S(2)}) async-start(), calls=%async_computation.4 | async-start | bytes 2621440 | tf_op jit(solution)/shard_map/psum | solution.py:111
  165.9 1.3 copy-start.8
  166.8 56.0 %copy-start.6 = (bf16[512,1280]{1,0:T(8,128)(2,1)S(1)}, bf16[512,1280]{1,0:T(8,128)(2,1)}, u32[]{:S(2)}) copy-start(bf16[512,1280]{1,0:T(8,128)(2,1)} %copy.62) | copy-start | bytes 3932164
  166.8 56.0 %copy-start.10 = (f32[1280]{0:T(1024)S(1)}, f32[1280]{0:T(1024)}, u32[]{:S(2)}) copy-start(f32[1280]{0:T(1024)} %param.26) | copy-start | bytes 15364
  169.1 57.0 %copy-start.11 = (f32[1280]{0:T(1024)S(1)}, f32[1280]{0:T(1024)}, u32[]{:S(2)}) copy-start(f32[1280]{0:T(1024)} %param.27) | copy-start | bytes 15364
  169.1 85.7 %all-gather.8.cloned.1.call-start = ((), (), s32[]{:S(2)}) async-start(), calls=%async_computation.6 | async-start | bytes 5324800 | tf_op jit(solution)/shard_map/all_gather | solution.py:119
  169.7 165.9 %all-gather.6.cloned.1.call-start = ((), (), s32[]{:S(2)}) async-start(), calls=%async_computation.5 | async-start | bytes 6656000 | tf_op jit(solution)/shard_map/all_gather | solution.py:118
  170.2 195.8 %reduce-scatter.2.cloned.1.call-start = ((), (), s32[]{:S(2)}) async-start(), calls=%async_computation.7 | async-start | bytes 1310720 | tf_op jit(solution)/shard_map/reduce_scatter | solution.py:125
  225.0 1.1 copy-start.7
  226.1 109.5 %copy-start.15 = (f32[640]{0:T(1024)S(1)}, f32[640]{0:T(1024)}, u32[]{:S(2)}) copy-start(f32[640]{0:T(1024)} %param.29) | copy-start | bytes 7684
  228.1 116.6 %copy-start.9 = (s32[512,16]{0,1:T(8,128)S(1)}, s32[512,16]{0,1:T(8,128)}, u32[]{:S(2)}) copy-start(s32[512,16]{0,1:T(8,128)} %param.21) | copy-start | bytes 98308
  228.1 137.9 %copy-start.13 = (f32[1024]{0:T(1024)S(1)}, f32[1024]{0:T(1024)}, u32[]{:S(2)}) copy-start(f32[1024]{0:T(1024)} %param.31) | copy-start | bytes 12292
  375.5 13.1 %copy-start.2 = (s32[512]{0:T(512)S(1)}, s32[512]{0:T(512)}, u32[]{:S(2)}) copy-start(s32[512]{0:T(512)} %param.19) | copy-start | bytes 6148
  375.5 13.7 %copy-start.5 = (s32[512]{0:T(512)S(1)}, s32[512]{0:T(512)}, u32[]{:S(2)}) copy-start(s32[512]{0:T(512)} %param.20) | copy-start | bytes 6148
  375.5 63.6 %all-to-all-start.1 = ((bf16[64,2,8192]{2,1,0:T(2,128)(2,1)}), bf16[64,2,8192]{2,1,0:T(2,128)(2,1)}, u32[]{:S(2)}, u32[]{:S(2)}) async-start(bf16[64,2,8192]{2,1,0:T(2,128)(2,1)} %reshape.416), calls=%async_computation.2 | async-start | bytes 4194304 | tf_op jit(solution)/shard_map/all_to_all | solution.py:147
  439.1 17.1 %copy-start.1 = (bf16[1280,3,320]{0,2,1:T(8,128)(2,1)S(1)}, bf16[1280,3,320]{0,2,1:T(8,128)(2,1)}, u32[]{:S(2)}) copy-start(bf16[1280,3,320]{0,2,1:T(8,128)(2,1)} %param.23) | copy-start | bytes 7372804
Sparse Core Ops, SparseCore 0:
  129.4 22.7 all-gather.3
  169.2 53.5 all-reduce.1
  344.9 21.0 reduce-scatter.1
Sparse Core Ops, SparseCore 1:
  172.3 82.4 all-gather.7
  257.3 78.2 all-gather.5
where the time goes:
time: 465 us; the launch traced here: 463 us
  waiting for transfers between devices  311 us (67%)
  local copies, waits for them, and re-layouts  66.3 us (14%)
  matrix products  28.4 us (6%)
  starting transfers between devices  26.2 us (6%)
  between operations  15.6 us (3%)
  other arithmetic  15.5 us (3%)
    all_gather x1, waiting for transfers between devices, per_device(): lax.all_gather(expand_weight, 'dp', axis=0, tiled=True)  80.8 us
    all_to_all x1, waiting for transfers between devices, per_device(): lax.all_to_all(outgoing, 'dp', split_axis=0, concat_axis=0, tiled=True)  61.3 us
    psum x1, waiting for transfers between devices, per_device(): lax.psum(partial_out.astype(jnp.bfloat16), 'tensor').astype(jnp.float32)  52.4 us
    all_to_all x1, waiting for transfers between devices, per_device(): lax.all_to_all(leaving, 'dp', split_axis=0, concat_axis=0, tiled=True)  46.6 us
    unnamed x43, local copies, waits for them, and re-layouts  43.5 us
    all_gather x1, waiting for transfers between devices, per_device(): lax.all_gather(output_weight, 'dp', axis=1, tiled=True)  26.7 us
    all_gather x1, waiting for transfers between devices, per_device(): full_rows = lax.all_gather(arrived, 'tensor', axis=1, tiled=True)  21.9 us
    reduce_scatter x1, waiting for transfers between devices, per_device(): lax.psum_scatter(spread.astype(jnp.bfloat16), 'tensor', scatter_dimension...  20.5 us
  transfers between devices with their start and end apart: 7, of which 7 were waited for; matrix products, arithmetic and copies ran while one was open for 2% of the time, Pallas kernels for 0%

commit v1 on v0

v1 whole, which is shorter than its diff:
```python
import functools
import math

import jax
import jax.numpy as jnp
from jax import lax
from jax.experimental import pallas as pl
from jax.experimental.pallas import tpu as pltpu
from jax.sharding import PartitionSpec as P

HD = 80
CAP = 64
LROWS = 160
NY, NZ, NC = 4, 8, 2
EPSILON = 1e-06
BF = jnp.bfloat16
F32 = jnp.float32
VMEM_BYTES = 40 * 1024 * 1024


def dot_tn(lhs, rhs):
    return lax.dot_general(lhs, rhs, (((0,), (0,)), ((), ())), preferred_element_type=F32)


def dot_nt(lhs, rhs):
    return lax.dot_general(lhs, rhs, (((1,), (1,)), ((), ())), preferred_element_type=F32)


def dot_nn(lhs, rhs):
    return jnp.dot(lhs, rhs, preferred_element_type=F32)


def params(**extra):
    return pltpu.CompilerParams(vmem_limit_bytes=VMEM_BYTES, **extra)


def whole(shape):
    return pl.BlockSpec(shape, lambda *_: (0,) * len(shape))


def attention_kernel(
    member_ref, a0, a1, a2, a3, gain, w_qkv, b_qkv, w_proj, key_tag, p0, p1, p2, p3, normed, context
):
    width, rows = normed.shape
    cols = width // 4
    heads = cols // HD
    member = member_ref[0]
    pieces = [ref[...].astype(F32) for ref in (a0, a1, a2, a3)]
    square = sum(jnp.sum(piece * piece, axis=0, keepdims=True) for piece in pieces)
    inverse = lax.rsqrt(square * (1.0 / width) + EPSILON)
    for shift, piece in enumerate(pieces):
        owner = lax.rem(member - shift + 4, 4)
        span = pl.ds(pl.multiple_of(owner * cols, 64), cols)
        normed[span, :] = (piece * inverse * gain[span, :]).astype(BF)
    qkv = (dot_nn(w_qkv[...], normed[...]) + b_qkv[...]).astype(BF)
    query_image = lax.broadcasted_iota(jnp.int32, (rows, rows), 1) // CAP + pl.program_id(0) * (
        rows // CAP
    )
    allowed = key_tag[...] == query_image
    for head in range(heads):
        query = qkv[head * HD : (head + 1) * HD]
        key = qkv[cols + head * HD : cols + (head + 1) * HD]
        value = qkv[2 * cols + head * HD : 2 * cols + (head + 1) * HD]
        scores = dot_tn(key, query) * (1.0 / math.sqrt(HD))
        scores = jnp.where(allowed, scores, -1e30)
        scores = jnp.exp(scores - jnp.max(scores, axis=0, keepdims=True))
        weights = (scores / jnp.sum(scores, axis=0, keepdims=True)).astype(BF)
        context[head * HD : (head + 1) * HD, :] = dot_nn(value, weights).astype(BF)
    for shift, out in enumerate((p0, p1, p2, p3)):
        owner = lax.rem(member + shift, 4)
        span = pl.ds(pl.multiple_of(owner * cols, 64), cols)
        out[...] = dot_nn(w_proj[span, :], context[...]).astype(BF)


def attention(member, pieces, gain, w_qkv, b_qkv, w_proj, key_tag, step_rows=256):
    cols, rows = pieces[0].shape
    width = cols * 4
    piece_spec = pl.BlockSpec((cols, step_rows), lambda i, *_: (0, i))
    return pl.pallas_call(
        attention_kernel,
        grid_spec=pltpu.PrefetchScalarGridSpec(
            num_scalar_prefetch=1,
            grid=(rows // step_rows,),
            in_specs=[piece_spec] * 4
            + [
                whole((width, 1)),
                whole((3 * cols, width)),
                whole((3 * cols, 1)),
                whole((width, cols)),
                pl.BlockSpec((step_rows, 1), lambda i, *_: (i, 0)),
            ],
            out_specs=[piece_spec] * 4,
            scratch_shapes=[
                pltpu.VMEM((width, step_rows), BF),
                pltpu.VMEM((cols, step_rows), BF),
            ],
        ),
        out_shape=[jax.ShapeDtypeStruct((cols, rows), BF)] * 4,
        compiler_params=params(),
        cost_estimate=pl.CostEstimate(
            flops=2 * rows * width * cols * 4, bytes_accessed=7 * 2**20, transcendentals=rows * 1024
        ),
        name="attention",
    )(member, *pieces, gain, w_qkv, b_qkv, w_proj, key_tag)


def expand_kernel(member_ref, e0, e1, e2, e3, gain, weight, bias, out, normed, total):
    width, rows = normed.shape
    cols = width // 4
    part = pl.program_id(0)
    member = member_ref[0]

    @pl.when(part == 0)
    def _():
        pieces = [ref[...].astype(F32) for ref in (e0, e1, e2, e3)]
        square = sum(jnp.sum(piece * piece, axis=0, keepdims=True) for piece in pieces)
        inverse = lax.rsqrt(square * (1.0 / width) + EPSILON)
        for shift, piece in enumerate(pieces):
            owner = lax.rem(member - shift + 4, 4)
            span = pl.ds(pl.multiple_of(owner * cols, 64), cols)
            normed[span, :] = (piece * inverse * gain[span, :]).astype(BF)
        total[...] = jnp.zeros_like(total)

    picks_shape = (rows // 4, rows)
    picks = (
        lax.broadcasted_iota(jnp.int32, picks_shape, 1)
        == 4 * lax.broadcasted_iota(jnp.int32, picks_shape, 0) + part
    )
    turned = dot_nt(picks.astype(F32).astype(BF), normed[...]).astype(BF)
    total[...] += dot_nn(turned, weight[...])

    @pl.when(part == 3)
    def _():
        value = total[...] + bias[...]
        out[...] = (0.5 * value * (1.0 + lax.erf(value * (1.0 / math.sqrt(2.0))))).astype(BF)


def expand(member, pieces, gain, weight, bias):
    cols, rows = pieces[0].shape
    width = cols * 4
    hidden = weight.shape[1]
    return pl.pallas_call(
        expand_kernel,
        grid_spec=pltpu.PrefetchScalarGridSpec(
            num_scalar_prefetch=1,
            grid=(4,),
            in_specs=[whole((cols, rows))] * 4
            + [
                whole((width, 1)),
                pl.BlockSpec((width, hidden), lambda i, *_: (i, 0)),
                whole((1, hidden)),
            ],
            out_specs=whole((rows // 4, hidden)),
            scratch_shapes=[
                pltpu.VMEM((width, rows), BF),
                pltpu.VMEM((rows // 4, hidden), F32),
            ],
        ),
        out_shape=jax.ShapeDtypeStruct((rows // 4, hidden), BF),
        compiler_params=params(),
        cost_estimate=pl.CostEstimate(
            flops=2 * rows * width * (hidden + rows // 4),
            bytes_accessed=9 * 2**20,
            transcendentals=rows // 4 * hidden,
        ),
        name="expand",
    )(member, *pieces, gain, weight, bias)


def route_kernel(*refs):
    source, blocks, outs, held = refs[0], refs[1:9], refs[9:17], refs[17]
    rows = blocks[0].shape[0]
    for at, block in enumerate(blocks):
        held[at * rows : (at + 1) * rows, :] = block[...]
    for at, out in enumerate(outs):
        wanted = source[at * rows : (at + 1) * rows, :]
        picks = lax.broadcasted_iota(jnp.int32, (rows, held.shape[0]), 1) == wanted
        out[...] = dot_nn(picks.astype(F32).astype(BF), held[...]).astype(BF)


def route(source, blocks):
    rows, hidden = blocks[0].shape
    return pl.pallas_call(
        route_kernel,
        out_shape=[jax.ShapeDtypeStruct((rows, hidden), BF)] * 8,
        scratch_shapes=[pltpu.VMEM((8 * rows, hidden), BF)],
        compiler_params=params(),
        cost_estimate=pl.CostEstimate(
            flops=2 * 64 * rows * rows * hidden, bytes_accessed=4 * 2**20, transcendentals=0
        ),
        name="route",
    )(source, *blocks)


def output_kernel(member_ref, *refs):
    blocks, weight, outs, held = refs[:8], refs[8], refs[9:13], refs[13]
    part = pl.program_id(0)

    @pl.when(part == 0)
    def _():
        held[...] = sum(block[...].astype(F32) for block in blocks).astype(BF)

    result = dot_nt(held[...], weight[...]).astype(BF)
    for at, out in enumerate(outs):

        @pl.when(part == at)
        def _(out=out):
            out[...] = result


def output_map(member, blocks, weight):
    rows, hidden = blocks[0].shape
    cols = weight.shape[0] // 4
    return pl.pallas_call(
        output_kernel,
        grid_spec=pltpu.PrefetchScalarGridSpec(
            num_scalar_prefetch=1,
            grid=(4,),
            in_specs=[whole((rows, hidden))] * 8
            + [pl.BlockSpec((cols, hidden), lambda i, member: (lax.rem(member[0] + i, 4), 0))],
            out_specs=[whole((rows, cols))] * 4,
            scratch_shapes=[pltpu.VMEM((rows, hidden), BF)],
        ),
        out_shape=[jax.ShapeDtypeStruct((rows, cols), BF)] * 4,
        compiler_params=params(),
        cost_estimate=pl.CostEstimate(
            flops=8 * rows * hidden * cols, bytes_accessed=8 * 2**20, transcendentals=0
        ),
        name="output_map",
    )(member, *blocks, weight)


def place_kernel(p0, p1, p2, p3, bias, source, out):
    total = sum(ref[...].astype(F32) for ref in (p0, p1, p2, p3)) + bias[...]
    rows = p0.shape[0]
    picks = lax.broadcasted_iota(jnp.int32, (out.shape[0], rows), 1) == source[...]
    out[...] = dot_nn(picks.astype(F32).astype(BF), total.astype(BF)).astype(BF)


def place(parts, bias, source):
    cols = parts[0].shape[1]
    return pl.pallas_call(
        place_kernel,
        out_shape=jax.ShapeDtypeStruct((source.shape[0], cols), BF),
        compiler_params=params(),
        name="place",
    )(*parts, bias, source)


def pack_kernel(slot_image, rows_ref, out, packed):
    half = rows_ref.shape[0] // 2
    for image in range(rows_ref.shape[1] // CAP):
        low = rows_ref[:half, image * CAP : (image + 1) * CAP]
        high = rows_ref[half:, image * CAP : (image + 1) * CAP]
        packed[image] = jnp.concatenate([low, high], axis=1)

    @pl.loop(0, out.shape[0])
    def _(slot):
        out[slot] = packed[slot_image[slot]]


def pack(slot_image, rows_t):
    half, images = rows_t.shape[0] // 2, rows_t.shape[1] // CAP
    slots = slot_image.shape[0]
    return pl.pallas_call(
        pack_kernel,
        in_specs=[pl.BlockSpec(memory_space=pltpu.SMEM), pl.BlockSpec(memory_space=pltpu.VMEM)],
        out_shape=jax.ShapeDtypeStruct((slots, half, 2 * CAP), BF),
        scratch_shapes=[pltpu.VMEM((images, half, 2 * CAP), BF)],
        compiler_params=params(),
        name="pack",
    )(slot_image, rows_t)


def unpack_kernel(slot_from, first, second, out):
    half = first.shape[1]
    out[:half, :] = jnp.concatenate([first[0, :, :CAP], second[0, :, :CAP]], axis=1)
    out[half:, :] = jnp.concatenate([first[0, :, CAP:], second[0, :, CAP:]], axis=1)


def unpack(slot_from, landed):
    half = landed.shape[1]
    images = slot_from.shape[0]
    return pl.pallas_call(
        unpack_kernel,
        grid_spec=pltpu.PrefetchScalarGridSpec(
            num_scalar_prefetch=1,
            grid=(images // 2,),
            in_specs=[
                pl.BlockSpec((1, half, 2 * CAP), lambda i, at: (at[2 * i], 0, 0)),
                pl.BlockSpec((1, half, 2 * CAP), lambda i, at: (at[2 * i + 1], 0, 0)),
            ],
            out_specs=pl.BlockSpec((2 * half, 2 * CAP), lambda i, at: (0, i)),
        ),
        out_shape=jax.ShapeDtypeStruct((2 * half, images * CAP), BF),
        compiler_params=params(),
        name="unpack",
    )(slot_from, landed, landed)


def tensor_shift(values, shift):
    return lax.ppermute(values, "tensor", [(i, (i + shift) % 4) for i in range(4)])


def rank_of(y, z, c):
    return ((y % NY) * NZ + z % NZ) * NC + c % NC


def dp_shift(values, dy, dz, dc):
    pairs = [
        (rank_of(y, z, c), rank_of(y + dy, z + dz, c + dc))
        for y in range(NY)
        for z in range(NZ)
        for c in range(NC)
    ]
    return lax.ppermute(values, "dp", pairs)


def per_device(
    patches,
    counts,
    source_slot,
    target_slot,
    lang_start,
    window_order,
    norm_gain,
    qkv_weight,
    qkv_bias,
    proj_weight,
    proj_bias,
    merge_gain,
    expand_weight,
    expand_bias,
    output_weight,
    output_bias,
):
    dp_index = lax.axis_index("dp")
    member = lax.axis_index("tensor")
    rows, cols = patches.shape
    images = rows // CAP
    depth = CAP // 4
    width = cols * 4
    at_y, at_z, at_c = dp_index // (NZ * NC), dp_index // NC % NZ, dp_index % NC
    member_arg = member.reshape(1).astype(jnp.int32)

    own = patches.T
    pieces = [own] + [tensor_shift(own, shift) for shift in (1, 2, 3)]
    expand_full = lax.all_gather(expand_weight, "dp", axis=0, tiled=True)
    output_full = lax.all_gather(output_weight.T, "dp", axis=0, tiled=True)

    slot_ids = dp_index * images + jnp.arange(images, dtype=jnp.int32)
    held = source_slot[None, :] == slot_ids[:, None]
    live_count = jnp.sum(jnp.where(held, counts[None, :], 0), axis=1)
    outward = jnp.sum(jnp.where(held, target_slot[None, :], 0), axis=1) // images
    bound = target_slot[None, :] == slot_ids[:, None]
    slot_from = jnp.sum(jnp.where(bound, source_slot[None, :], 0), axis=1) // images
    rank_ids = jnp.arange(NY * NZ * NC, dtype=jnp.int32)
    slot_image = jnp.sum(
        jnp.where(
            outward[None, :] == rank_ids[:, None], jnp.arange(images, dtype=jnp.int32)[None, :], 0
        ),
        axis=1,
    )
    row_ids = jnp.arange(CAP, dtype=jnp.int32)
    live = row_ids[None, :] < live_count[:, None]
    image_ids = jnp.arange(images, dtype=jnp.int32)
    key_tag = jnp.where(live, image_ids[:, None], -1).reshape(rows, 1)
    live_row = live.reshape(1, rows)

    def plane(table):
        tail = table.shape[1:]
        table = table.reshape(NY, NZ, NC, images, *tail)
        table = lax.dynamic_index_in_dim(table, at_z, 1, keepdims=False)
        table = lax.dynamic_slice_in_dim(jnp.concatenate([table, table], 0), at_y, NY, 0)
        return lax.dynamic_slice_in_dim(jnp.concatenate([table, table], 1), at_c, NC, 1)

    plane_source = plane(source_slot)
    plane_rank = plane_source // images
    here = jnp.logical_and(plane_rank // (NZ * NC) == at_y, plane_rank % NC == at_c)
    step = (at_z - plane_rank // NC % NZ + NZ) % NZ
    base = (step * images + plane_source % images) * depth
    route_source = jnp.where(here[..., None], base[..., None] + plane(window_order), -1)
    route_source = route_source.reshape(NY * NC * images * depth, 1)

    own_start = (
        lax.dynamic_slice_in_dim(lang_start, dp_index * images, images, 0) - dp_index * LROWS
    )
    own_used = lax.dynamic_slice_in_dim(counts, dp_index * images, images, 0) // 4
    lang_rows = jnp.arange(LROWS, dtype=jnp.int32)[:, None]
    inside = jnp.logical_and(
        lang_rows >= own_start[None, :], lang_rows < own_start[None, :] + own_used[None, :]
    )
    place_source = (
        jnp.sum(
            jnp.where(inside, image_ids[None, :] * depth + lang_rows - own_start[None, :] + 1, 0),
            axis=1,
            keepdims=True,
        )
        - 1
    )

    parts = attention(
        member_arg,
        pieces,
        norm_gain.reshape(width, 1),
        qkv_weight.transpose(1, 2, 0).reshape(3 * cols, width),
        qkv_bias.reshape(3 * cols, 1),
        proj_weight.T,
        key_tag,
    )
    arrived = [tensor_shift(parts[shift], shift) for shift in (1, 2, 3)]
    summed = sum(part.astype(F32) for part in [parts[0]] + arrived)
    own_bias = lax.dynamic_slice_in_dim(proj_bias, member * cols, cols, 0)
    hidden = own.astype(F32) + summed + own_bias[:, None]
    encoded_here = jnp.where(live_row, hidden, 0.0).astype(BF)

    encoded_pieces = [encoded_here] + [tensor_shift(encoded_here, shift) for shift in (1, 2, 3)]
    leaving = pack(slot_image, encoded_here)
    landed = lax.all_to_all(leaving, "dp", split_axis=0, concat_axis=0, tiled=True)

    expanded = expand(
        member_arg,
        encoded_pieces,
        merge_gain.reshape(width, 1),
        expand_full,
        expand_bias.reshape(1, -1),
    )
    ring = [expanded] + [dp_shift(expanded, 0, shift, 0) for shift in range(1, NZ)]
    routed = route(route_source, ring)
    blocks = [routed[0]]
    for at in range(1, NY * NC):
        blocks.append(dp_shift(routed[at], at // NC, 0, at % NC))
    out_parts = output_map(member_arg, blocks, output_full)
    out_arrived = [tensor_shift(out_parts[shift], shift) for shift in (1, 2, 3)]
    merged = place([out_parts[0]] + out_arrived, output_bias.reshape(1, -1), place_source)
    encoded = unpack(slot_from, landed).T
    return (encoded, merged)


def solution(mesh):
    in_specs = (
        P("dp", "tensor"),
        P(),
        P(),
        P(),
        P(),
        P(),
        P(),
        P(None, None, "tensor"),
        P(None, "tensor"),
        P("tensor", None),
        P(),
        P(),
        P("dp", "tensor"),
        P("tensor"),
        P("tensor", "dp"),
        P("tensor"),
    )
    out_specs = (P("dp", "tensor"), P("dp", "tensor"))
    return jax.shard_map(
        per_device, mesh=mesh, in_specs=in_specs, out_specs=out_specs, check_vma=False
    )
```

time: 465 us -> 251 us (0.54)
  waiting for transfers between devices: 311 us -> 123 us
  local copies, waits for them, and re-layouts: 66.3 us -> 32.7 us
  matrix products: 28.4 us -> 0 us
  Pallas kernels: 0 us -> 25.4 us
  starting transfers between devices: 26.2 us -> 50.7 us
  other arithmetic: 15.5 us -> 2.53 us
    all_gather x3 -> x2, waiting for transfers between devices: 129 us -> 39.4 us  [the longest x1 22.3 us: per_device(): expand_full = lax.all_gather(expand_weight, 'dp', axis=0, tiled=True)]
    ppermute x0 -> x26, waiting for transfers between devices: none -> 81.9 us  [the longest x12 43.5 us: tensor_shift(): lax.ppermute(values, 'tensor', [(i, (i + shift) % 4) for i in range(4)])]
    all_to_all x1 -> x0, waiting for transfers between devices: 61.3 us -> none  [per_device(): lax.all_to_all(outgoing, 'dp', split_axis=0, concat_axis=0, tiled=True)]
    psum x1 -> x0, waiting for transfers between devices: 52.4 us -> none  [per_device(): lax.psum(partial_out.astype(jnp.bfloat16), 'tensor').astype(jnp.float32)]
    all_to_all x1, waiting for transfers between devices: 46.6 us -> 0.01 us  [per_device(): lax.all_to_all(leaving, 'dp', split_axis=0, concat_axis=0, tiled=True)]
    ppermute x0 -> x26, starting transfers between devices: none -> 37.3 us  [the longest x14 19.1 us: dp_shift(): return lax.ppermute(values, 'dp', pairs)]
    dot_general x10 -> x0, matrix products: 27.9 us -> none  [the longest x2 9.83 us: take_rows(): jnp.dot(picks, payload, preferred_element_type=jnp.float32)]
    pallas_call x0 -> x7, Pallas kernels: none -> 25.4 us  [the longest x1 8.36 us: attention(): pl.pallas_call(attention_kernel, grid_spec=pltpu.PrefetchScalarGridSpec(n...]
  transfers between devices with their start and end apart: 7 -> 29, of which waited for: 7 -> 14; matrix products, arithmetic and copies ran while one was open for 2% -> 4% of each run, Pallas kernels for 0% -> 9%
where the time goes in v1:
time: 251 us; the launch traced here: 248 us
  waiting for transfers between devices  123 us (49%)
  starting transfers between devices  50.7 us (20%)
  local copies, waits for them, and re-layouts  32.7 us (13%)
  Pallas kernels  25.4 us (10%)
  between operations  14.4 us (6%)
  other arithmetic  2.53 us (1%)
    ppermute x12, waiting for transfers between devices, tensor_shift(): lax.ppermute(values, 'tensor', [(i, (i + shift) % 4) for i in range(4)])  43.5 us
    ppermute x14, waiting for transfers between devices, dp_shift(): return lax.ppermute(values, 'dp', pairs)  38.3 us
    unnamed x68, local copies, waits for them, and re-layouts  27.2 us
    all_gather x1, waiting for transfers between devices, per_device(): expand_full = lax.all_gather(expand_weight, 'dp', axis=0, tiled=True)  22.3 us
    ppermute x14, starting transfers between devices, dp_shift(): return lax.ppermute(values, 'dp', pairs)  19.1 us
    ppermute x12, starting transfers between devices, tensor_shift(): lax.ppermute(values, 'tensor', [(i, (i + shift) % 4) for i in range(4)])  18.3 us
    all_gather x1, waiting for transfers between devices, per_device(): output_full = lax.all_gather(output_weight.T, 'dp', axis=0, tiled=True)  17.1 us
    all_to_all x1, starting transfers between devices, per_device(): lax.all_to_all(leaving, 'dp', split_axis=0, concat_axis=0, tiled=True)  13.3 us
  transfers between devices with their start and end apart: 29, of which 14 were waited for; matrix products, arithmetic and copies ran while one was open for 4% of the time, Pallas kernels for 9%

profile of v1, /device:TPU:1, one launch (start us, length us, event | category | flops | bytes accessed | tf_op | source)
XLA Modules:
  0.0 248.3 jit_solution(15370289017381928466)
XLA Ops:
  8.7 2.1 collective-permute-start
  10.8 2.5 collective-permute-start.1
  15.6 2.2 copy.28
  20.9 6.8 %collective-permute-done.1.a2 = bf16[320,512]{1,0:T(8,128)(2,1)} collective-permute-done((bf16[320,512]{1,0:T(8,128)(2,1)}, bf16[320,512]{1,0:T(8,128)(2,1)}, u32[]{:S(2)}, u32[]{:S(2)}) %collective-permute-start.1) | collective-permute-done | bytes 327712 | tf_op jit(solution)/shard_map/ppermute | solution.py:302
  30.9 8.4 %attention.1 = (bf16[320,512]{1,0:T(8,128)(2,1)S(1)}, bf16[320,512]{1,0:T(8,128)(2,1)S(1)}, bf16[320,512]{1,0:T(8,128)(2,1)S(1)}, bf16[320,512]{1,0:T(8,128)(2,1)S(1)}) custom-call(s32[1]{0:T(128)} %bitcast.1.member_ref, bf16[320,512]{1,0:T(8,128)(2,1)S(1)} %bitcast.22, bf16[320,512]{1,0:T(8,128)(2,1)} %collective-permute-done.a1, ...), custom_call_target="tpu_custom_call" | custom-call | flops 1677721600 | bytes 7340032 | tf_op jit(solution)/shard_map/attention/pallas_call | solution.py:79
  40.5 3.0 %collective-permute-start.4 = (bf16[320,512]{1,0:T(8,128)(2,1)S(1)}, bf16[320,512]{1,0:T(8,128)(2,1)S(1)}, u32[]{:S(2)}, u32[]{:S(2)}) collective-permute-start(bf16[320,512]{1,0:T(8,128)(2,1)S(1)} %get-tuple-element.20), channel_id=1, source_target_pairs={{0,2},{1,3},{2,0},{3,1},{4,6},{5,7},{6,4},{7,5},{8,10},{9,11},{10,... | collective-permute-start | bytes 983048 | tf_op jit(solution)/shard_map/ppermute | solution.py:302
  43.6 5.2 %collective-permute-done.3 = bf16[320,512]{1,0:T(8,128)(2,1)S(1)} collective-permute-done((bf16[320,512]{1,0:T(8,128)(2,1)S(1)}, bf16[320,512]{1,0:T(8,128)(2,1)S(1)}, u32[]{:S(2)}, u32[]{:S(2)}) %collective-permute-start.3) | collective-permute-done | bytes 327712 | tf_op jit(solution)/shard_map/ppermute | solution.py:302
  48.8 9.0 %collective-permute-done.4 = bf16[320,512]{1,0:T(8,128)(2,1)S(1)} collective-permute-done((bf16[320,512]{1,0:T(8,128)(2,1)S(1)}, bf16[320,512]{1,0:T(8,128)(2,1)S(1)}, u32[]{:S(2)}, u32[]{:S(2)}) %collective-permute-start.4) | collective-permute-done | bytes 327712 | tf_op jit(solution)/shard_map/ppermute | solution.py:302
  60.8 13.3 %all-to-all-start = ((bf16[64,160,128]{2,1,0:T(8,128)(2,1)}), bf16[64,160,128]{2,1,0:T(8,128)(2,1)S(1)}, u32[]{:S(2)}, u32[]{:S(2)}) async-start(bf16[64,160,128]{2,1,0:T(8,128)(2,1)} %copy-done), calls=%async_computation | async-start | bytes 5242880 | tf_op jit(solution)/shard_map/all_to_all | solution.py:419
  76.8 2.6 %collective-permute-start.7 = (bf16[320,512]{1,0:T(8,128)(2,1)S(1)}, bf16[320,512]{1,0:T(8,128)(2,1)S(1)}, u32[]{:S(2)}, u32[]{:S(2)}) collective-permute-start(bf16[320,512]{1,0:T(8,128)(2,1)S(1)} %select_convert_fusion.rows_ref.e0), channel_id=1, source_target_pairs={{0,2},{1,3},{2,0},{3,1},{4,6},{5,7},{6,4},{7,5},{8,10},{9,11},{10,... | collective-permute-start | bytes 983048 | tf_op jit(solution)/shard_map/ppermute | solution.py:302
  79.6 6.8 %collective-permute-done.6.e1 = bf16[320,512]{1,0:T(8,128)(2,1)S(1)} collective-permute-done((bf16[320,512]{1,0:T(8,128)(2,1)S(1)}, bf16[320,512]{1,0:T(8,128)(2,1)S(1)}, u32[]{:S(2)}, u32[]{:S(2)}) %collective-permute-start.6) | collective-permute-done | bytes 327712 | tf_op jit(solution)/shard_map/ppermute | solution.py:302
  86.5 7.3 %collective-permute-done.7.e2 = bf16[320,512]{1,0:T(8,128)(2,1)S(1)} collective-permute-done((bf16[320,512]{1,0:T(8,128)(2,1)S(1)}, bf16[320,512]{1,0:T(8,128)(2,1)S(1)}, u32[]{:S(2)}, u32[]{:S(2)}) %collective-permute-start.7) | collective-permute-done | bytes 327712 | tf_op jit(solution)/shard_map/ppermute | solution.py:302
  95.2 22.3 %all-gather.3.cloned.1.call-done.weight = bf16[5120,640]{1,0:T(8,128)(2,1)} async-done(((bf16[80,640]{1,0:T(8,128)(2,1)}), bf16[5120,640]{1,0:T(8,128)(2,1)}) %all-gather.3.cloned.1.call-update) | async-done | bytes 6553616 | tf_op jit(solution)/shard_map/all_gather | solution.py:348
  117.5 2.9 %copy-done.1 = bf16[5120,640]{1,0:T(8,128)(2,1)S(1)} copy-done((bf16[5120,640]{1,0:T(8,128)(2,1)S(1)}, bf16[5120,640]{1,0:T(8,128)(2,1)}, u32[]{:S(2)}) %copy-start.1) | copy-done | bytes 6553624
  123.4 4.2 %expand.1.refs_1_ = bf16[128,640]{1,0:T(8,128)(2,1)S(1)} custom-call(s32[1]{0:T(128)} %bitcast.1.member_ref, bf16[320,512]{1,0:T(8,128)(2,1)S(1)} %select_convert_fusion.rows_ref.e0, bf16[320,512]{1,0:T(8,128)(2,1)S(1)} %collective-permute-done.6.e1, bf16[320,512]{1,0:T(8,128)(2,1)S(1)} %copy-done.7, bf16[320,512]{1,0:T(8,128)(2,1)S(1)} %copy-done.9, ...), custom_call_target="tpu_custom_call" | custom-call | flops 1006632960 | bytes 9437184 | tf_op jit(solution)/shard_map/expand/pallas_call | solution.py:142
  127.7 3.1 %collective-permute-start.11 = (bf16[128,640]{1,0:T(8,128)(2,1)S(1)}, bf16[128,640]{1,0:T(8,128)(2,1)S(1)}, u32[]{:S(2)}, u32[]{:S(2)}) collective-permute-start(bf16[128,640]{1,0:T(8,128)(2,1)S(1)} %expand.1.refs_1_), channel_id=1, source_target_pairs={{0,24},{4,28},{8,32},{12,36},{16,40},{20,44},{24,48},{28,52},{32,5... | collective-permute-start | bytes 491528 | tf_op jit(solution)/shard_map/ppermute | solution.py:316
  133.0 3.2 %collective-permute-start.13 = (bf16[128,640]{1,0:T(8,128)(2,1)S(1)}, bf16[128,640]{1,0:T(8,128)(2,1)}, u32[]{:S(2)}, u32[]{:S(2)}) collective-permute-start(bf16[128,640]{1,0:T(8,128)(2,1)S(1)} %expand.1.refs_1_), channel_id=1, source_target_pairs={{0,40},{4,44},{8,48},{12,52},{16,56},{20,60},{24,0},{28,4},{32,8},... | collective-permute-start | bytes 491528 | tf_op jit(solution)/shard_map/ppermute | solution.py:316
  136.2 2.4 collective-permute-start.14
  138.6 14.5 %collective-permute-done.10.refs_3_ = bf16[128,640]{1,0:T(8,128)(2,1)S(1)} collective-permute-done((bf16[128,640]{1,0:T(8,128)(2,1)S(1)}, bf16[128,640]{1,0:T(8,128)(2,1)S(1)}, u32[]{:S(2)}, u32[]{:S(2)}) %collective-permute-start.10) | collective-permute-done | bytes 163872 | tf_op jit(solution)/shard_map/ppermute | solution.py:316
  153.9 11.9 %collective-permute-done.11.refs_4_ = bf16[128,640]{1,0:T(8,128)(2,1)S(1)} collective-permute-done((bf16[128,640]{1,0:T(8,128)(2,1)S(1)}, bf16[128,640]{1,0:T(8,128)(2,1)S(1)}, u32[]{:S(2)}, u32[]{:S(2)}) %collective-permute-start.11) | collective-permute-done | bytes 163872 | tf_op jit(solution)/shard_map/ppermute | solution.py:316
  167.0 5.6 %collective-permute-done.12.refs_5_ = bf16[128,640]{1,0:T(8,128)(2,1)S(1)} collective-permute-done((bf16[128,640]{1,0:T(8,128)(2,1)S(1)}, bf16[128,640]{1,0:T(8,128)(2,1)S(1)}, u32[]{:S(2)}, u32[]{:S(2)}) %collective-permute-start.12) | collective-permute-done | bytes 163872 | tf_op jit(solution)/shard_map/ppermute | solution.py:316
  173.2 2.9 %collective-permute-done.9.refs_2_ = bf16[128,640]{1,0:T(8,128)(2,1)} collective-permute-done((bf16[128,640]{1,0:T(8,128)(2,1)S(1)}, bf16[128,640]{1,0:T(8,128)(2,1)}, u32[]{:S(2)}, u32[]{:S(2)}) %collective-permute-start.9) | collective-permute-done | bytes 163872 | tf_op jit(solution)/shard_map/ppermute | solution.py:316
  178.9 3.0 %route.1 = (bf16[128,640]{1,0:T(8,128)(2,1)S(1)}, bf16[128,640]{1,0:T(8,128)(2,1)}, bf16[128,640]{1,0:T(8,128)(2,1)}, bf16[128,640]{1,0:T(8,128)(2,1)S(1)}, bf16...) custom-call(s32[1024,1]{1,0:T(8,128)S(1)} %reshape.144.refs_0_, ...), custom_call_target="tpu_custom_call" | custom-call | flops 1342177280 | bytes 4194304 | tf_op jit(solution)/shard_map/route/pallas_call | solution.py:183
  186.3 2.2 collective-permute-start.19
  190.7 3.3 %collective-permute-done.17.refs_2_ = bf16[128,640]{1,0:T(8,128)(2,1)S(1)} collective-permute-done((bf16[128,640]{1,0:T(8,128)(2,1)}, bf16[128,640]{1,0:T(8,128)(2,1)S(1)}, u32[]{:S(2)}, u32[]{:S(2)}) %collective-permute-start.17) | collective-permute-done | bytes 163872 | tf_op jit(solution)/shard_map/ppermute | solution.py:316
  196.5 17.1 %all-gather.5.cloned.1.call-done.refs_8_ = bf16[4096,640]{1,0:T(8,128)(2,1)} async-done(((bf16[64,640]{1,0:T(8,128)(2,1)}), bf16[4096,640]{1,0:T(8,128)(2,1)}) %all-gather.5.cloned.1.call-update) | async-done | bytes 5242896 | tf_op jit(solution)/shard_map/all_gather | solution.py:349
  215.0 2.5 copy-done.2
  219.3 4.5 %output_map.1 = (bf16[128,1024]{1,0:T(8,128)(2,1)S(1)}, bf16[128,1024]{1,0:T(8,128)(2,1)}, bf16[128,1024]{1,0:T(8,128)(2,1)}, bf16[128,1024]{1,0:T(8,128)(2,1)}) custom-call(s32[1]{0:T(128)} %bitcast.1.member_ref, bf16[128,640]{1,0:T(8,128)(2,1)S(1)} %get-tuple-element.22.refs_0_, bf16[128,640]{1,0:T(8,128)(2,1)S(1)} %collective-permute-done.16.refs_1_, ...), custom_call_target="tpu_custom_call" | custom-call | flops 671088640 | bytes 8388608 | tf_op jit(solution)/shard_map/output_map/pallas_call | solution.py:214
  225.1 2.3 collective-permute-start.24
  229.0 2.1 unpack.1
  232.9 6.6 %collective-permute-done.24.p2 = bf16[128,1024]{1,0:T(8,128)(2,1)S(1)} collective-permute-done((bf16[128,1024]{1,0:T(8,128)(2,1)}, bf16[128,1024]{1,0:T(8,128)(2,1)S(1)}, u32[]{:S(2)}, u32[]{:S(2)}) %collective-permute-start.24) | collective-permute-done | bytes 262176 | tf_op jit(solution)/shard_map/ppermute | solution.py:302
  239.5 2.0 place.1
  (131 shorter events, 46.2 us)
Async XLA Ops:
  7.2 20.5 %copy-start.16 = (bf16[1280,3,320]{0,2,1:T(8,128)(2,1)S(1)}, bf16[1280,3,320]{0,2,1:T(8,128)(2,1)}, u32[]{:S(2)}) copy-start(bf16[1280,3,320]{0,2,1:T(8,128)(2,1)} %param.23) | copy-start | bytes 7372804
  7.2 110.4 %all-gather.3.cloned.1.call-start = ((), (), s32[]{:S(2)}) async-start(), calls=%async_computation.1 | async-start | bytes 6656000 | tf_op jit(solution)/shard_map/all_gather | solution.py:348
  7.9 205.7 %all-gather.5.cloned.1.call-start = ((), (), s32[]{:S(2)}) async-start(), calls=%async_computation.2 | async-start | bytes 5324800 | tf_op jit(solution)/shard_map/all_gather | solution.py:349
  8.7 12.2 %collective-permute-start = (bf16[320,512]{1,0:T(8,128)(2,1)}, bf16[320,512]{1,0:T(8,128)(2,1)}, u32[]{:S(2)}, u32[]{:S(2)}) collective-permute-start(bf16[320,512]{1,0:T(8,128)(2,1)} %bitcast.19), channel_id=1, source_target_pairs={{0,1},{1,2},{2,3},{3,0},{4,5},{5,6},{6,7},{7,4},{8,9},{9,10},{10,1... | collective-permute-start | bytes 983048 | tf_op jit(solution)/shard_map/ppermute | solution.py:302
  10.8 16.9 %collective-permute-start.1 = (bf16[320,512]{1,0:T(8,128)(2,1)}, bf16[320,512]{1,0:T(8,128)(2,1)}, u32[]{:S(2)}, u32[]{:S(2)}) collective-permute-start(bf16[320,512]{1,0:T(8,128)(2,1)} %bitcast.20), channel_id=1, source_target_pairs={{0,2},{1,3},{2,0},{3,1},{4,6},{5,7},{6,4},{7,5},{8,10},{9,11},{10,... | collective-permute-start | bytes 983048 | tf_op jit(solution)/shard_map/ppermute | solution.py:302
  13.2 14.5 %collective-permute-start.2 = (bf16[320,512]{1,0:T(8,128)(2,1)}, bf16[320,512]{1,0:T(8,128)(2,1)}, u32[]{:S(2)}, u32[]{:S(2)}) collective-permute-start(bf16[320,512]{1,0:T(8,128)(2,1)} %bitcast.21), channel_id=1, source_target_pairs={{0,3},{1,0},{2,1},{3,2},{4,7},{5,4},{6,5},{7,6},{8,11},{9,8},{10,9... | collective-permute-start | bytes 983048 | tf_op jit(solution)/shard_map/ppermute | solution.py:302
  39.3 9.5 %collective-permute-start.3 = (bf16[320,512]{1,0:T(8,128)(2,1)S(1)}, bf16[320,512]{1,0:T(8,128)(2,1)S(1)}, u32[]{:S(2)}, u32[]{:S(2)}) collective-permute-start(bf16[320,512]{1,0:T(8,128)(2,1)S(1)} %get-tuple-element.19), channel_id=1, source_target_pairs={{0,1},{1,2},{2,3},{3,0},{4,5},{5,6},{6,7},{7,4},{8,9},{9,10},{10,1... | collective-permute-start | bytes 983048 | tf_op jit(solution)/shard_map/ppermute | solution.py:302
  40.5 17.3 %collective-permute-start.4 = (bf16[320,512]{1,0:T(8,128)(2,1)S(1)}, bf16[320,512]{1,0:T(8,128)(2,1)S(1)}, u32[]{:S(2)}, u32[]{:S(2)}) collective-permute-start(bf16[320,512]{1,0:T(8,128)(2,1)S(1)} %get-tuple-element.20), channel_id=1, source_target_pairs={{0,2},{1,3},{2,0},{3,1},{4,6},{5,7},{6,4},{7,5},{8,10},{9,11},{10,... | collective-permute-start | bytes 983048 | tf_op jit(solution)/shard_map/ppermute | solution.py:302
  43.5 14.3 %collective-permute-start.5 = (bf16[320,512]{1,0:T(8,128)(2,1)S(1)}, bf16[320,512]{1,0:T(8,128)(2,1)S(1)}, u32[]{:S(2)}, u32[]{:S(2)}) collective-permute-start(bf16[320,512]{1,0:T(8,128)(2,1)S(1)} %get-tuple-element.21), channel_id=1, source_target_pairs={{0,3},{1,0},{2,1},{3,2},{4,7},{5,4},{6,5},{7,6},{8,11},{9,8},{10,9... | collective-permute-start | bytes 983048 | tf_op jit(solution)/shard_map/ppermute | solution.py:302
  60.8 14.6 %copy-start.32 = (f32[640]{0:T(1024)S(1)}, f32[640]{0:T(1024)}, u32[]{:S(2)}) copy-start(f32[640]{0:T(1024)} %param.29) | copy-start | bytes 7684
  60.8 14.6 %copy-start.28 = (s32[512,16]{0,1:T(8,128)S(1)}, s32[512,16]{0,1:T(8,128)}, u32[]{:S(2)}) copy-start(s32[512,16]{0,1:T(8,128)} %param.21) | copy-start | bytes 98308
  60.8 168.2 %all-to-all-start = ((bf16[64,160,128]{2,1,0:T(8,128)(2,1)}), bf16[64,160,128]{2,1,0:T(8,128)(2,1)S(1)}, u32[]{:S(2)}, u32[]{:S(2)}) async-start(bf16[64,160,128]{2,1,0:T(8,128)(2,1)} %copy-done), calls=%async_computation | async-start | bytes 5242880 | tf_op jit(solution)/shard_map/all_to_all | solution.py:419
  76.2 10.2 %collective-permute-start.6 = (bf16[320,512]{1,0:T(8,128)(2,1)S(1)}, bf16[320,512]{1,0:T(8,128)(2,1)S(1)}, u32[]{:S(2)}, u32[]{:S(2)}) collective-permute-start(bf16[320,512]{1,0:T(8,128)(2,1)S(1)} %select_convert_fusion.rows_ref.e0), channel_id=1, source_target_pairs={{0,1},{1,2},{2,3},{3,0},{4,5},{5,6},{6,7},{7,4},{8,9},{9,10},{10,1... | collective-permute-start | bytes 983048 | tf_op jit(solution)/shard_map/ppermute | solution.py:302
  76.8 17.0 %collective-permute-start.7 = (bf16[320,512]{1,0:T(8,128)(2,1)S(1)}, bf16[320,512]{1,0:T(8,128)(2,1)S(1)}, u32[]{:S(2)}, u32[]{:S(2)}) collective-permute-start(bf16[320,512]{1,0:T(8,128)(2,1)S(1)} %select_convert_fusion.rows_ref.e0), channel_id=1, source_target_pairs={{0,2},{1,3},{2,0},{3,1},{4,6},{5,7},{6,4},{7,5},{8,10},{9,11},{10,... | collective-permute-start | bytes 983048 | tf_op jit(solution)/shard_map/ppermute | solution.py:302
  79.4 15.1 %collective-permute-start.8 = (bf16[320,512]{1,0:T(8,128)(2,1)S(1)}, bf16[320,512]{1,0:T(8,128)(2,1)S(1)}, u32[]{:S(2)}, u32[]{:S(2)}) collective-permute-start(bf16[320,512]{1,0:T(8,128)(2,1)S(1)} %select_convert_fusion.rows_ref.e0), channel_id=1, source_target_pairs={{0,3},{1,0},{2,1},{3,2},{4,7},{5,4},{6,5},{7,6},{8,11},{9,8},{10,9... | collective-permute-start | bytes 983048 | tf_op jit(solution)/shard_map/ppermute | solution.py:302
  127.6 25.6 %collective-permute-start.10 = (bf16[128,640]{1,0:T(8,128)(2,1)S(1)}, bf16[128,640]{1,0:T(8,128)(2,1)S(1)}, u32[]{:S(2)}, u32[]{:S(2)}) collective-permute-start(bf16[128,640]{1,0:T(8,128)(2,1)S(1)} %expand.1.refs_1_), channel_id=1, source_target_pairs={{0,16},{4,20},{8,24},{12,28},{16,32},{20,36},{24,40},{28,44},{32,4... | collective-permute-start | bytes 491528 | tf_op jit(solution)/shard_map/ppermute | solution.py:316
  127.7 38.2 %collective-permute-start.11 = (bf16[128,640]{1,0:T(8,128)(2,1)S(1)}, bf16[128,640]{1,0:T(8,128)(2,1)S(1)}, u32[]{:S(2)}, u32[]{:S(2)}) collective-permute-start(bf16[128,640]{1,0:T(8,128)(2,1)S(1)} %expand.1.refs_1_), channel_id=1, source_target_pairs={{0,24},{4,28},{8,32},{12,36},{16,40},{20,44},{24,48},{28,52},{32,5... | collective-permute-start | bytes 491528 | tf_op jit(solution)/shard_map/ppermute | solution.py:316
  131.5 41.0 %collective-permute-start.12 = (bf16[128,640]{1,0:T(8,128)(2,1)S(1)}, bf16[128,640]{1,0:T(8,128)(2,1)S(1)}, u32[]{:S(2)}, u32[]{:S(2)}) collective-permute-start(bf16[128,640]{1,0:T(8,128)(2,1)S(1)} %expand.1.refs_1_), channel_id=1, source_target_pairs={{0,32},{4,36},{8,40},{12,44},{16,48},{20,52},{24,56},{28,60},{32,0... | collective-permute-start | bytes 491528 | tf_op jit(solution)/shard_map/ppermute | solution.py:316
  133.0 40.3 %collective-permute-start.13 = (bf16[128,640]{1,0:T(8,128)(2,1)S(1)}, bf16[128,640]{1,0:T(8,128)(2,1)}, u32[]{:S(2)}, u32[]{:S(2)}) collective-permute-start(bf16[128,640]{1,0:T(8,128)(2,1)S(1)} %expand.1.refs_1_), channel_id=1, source_target_pairs={{0,40},{4,44},{8,48},{12,52},{16,56},{20,60},{24,0},{28,4},{32,8},... | collective-permute-start | bytes 491528 | tf_op jit(solution)/shard_map/ppermute | solution.py:316
  136.2 37.1 %collective-permute-start.14 = (bf16[128,640]{1,0:T(8,128)(2,1)S(1)}, bf16[128,640]{1,0:T(8,128)(2,1)}, u32[]{:S(2)}, u32[]{:S(2)}) collective-permute-start(bf16[128,640]{1,0:T(8,128)(2,1)S(1)} %expand.1.refs_1_), channel_id=1, source_target_pairs={{0,48},{4,52},{8,56},{12,60},{16,0},{20,4},{24,8},{28,12},{32,16},... | collective-permute-start | bytes 491528 | tf_op jit(solution)/shard_map/ppermute | solution.py:316
  153.8 19.4 %collective-permute-start.15 = (bf16[128,640]{1,0:T(8,128)(2,1)S(1)}, bf16[128,640]{1,0:T(8,128)(2,1)}, u32[]{:S(2)}, u32[]{:S(2)}) collective-permute-start(bf16[128,640]{1,0:T(8,128)(2,1)S(1)} %expand.1.refs_1_), channel_id=1, source_target_pairs={{0,56},{4,60},{8,0},{12,4},{16,8},{20,12},{24,16},{28,20},{32,24},... | collective-permute-start | bytes 491528 | tf_op jit(solution)/shard_map/ppermute | solution.py:316
  166.6 9.6 %collective-permute-start.9 = (bf16[128,640]{1,0:T(8,128)(2,1)S(1)}, bf16[128,640]{1,0:T(8,128)(2,1)}, u32[]{:S(2)}, u32[]{:S(2)}) collective-permute-start(bf16[128,640]{1,0:T(8,128)(2,1)S(1)} %expand.1.refs_1_), channel_id=1, source_target_pairs={{0,8},{4,12},{8,16},{12,20},{16,24},{20,28},{24,32},{28,36},{32,40... | collective-permute-start | bytes 491528 | tf_op jit(solution)/shard_map/ppermute | solution.py:316
  183.2 5.8 %collective-permute-start.16 = (bf16[128,640]{1,0:T(8,128)(2,1)}, bf16[128,640]{1,0:T(8,128)(2,1)S(1)}, u32[]{:S(2)}, u32[]{:S(2)}) collective-permute-start(bf16[128,640]{1,0:T(8,128)(2,1)} %get-tuple-element.23), channel_id=1, source_target_pairs={{0,4},{4,0},{8,12},{12,8},{16,20},{20,16},{24,28},{28,24},{32,36},... | collective-permute-start | bytes 491528 | tf_op jit(solution)/shard_map/ppermute | solution.py:316
  184.0 9.9 %collective-permute-start.17 = (bf16[128,640]{1,0:T(8,128)(2,1)}, bf16[128,640]{1,0:T(8,128)(2,1)S(1)}, u32[]{:S(2)}, u32[]{:S(2)}) collective-permute-start(bf16[128,640]{1,0:T(8,128)(2,1)} %get-tuple-element.24), channel_id=1, source_target_pairs={{0,64},{4,68},{8,72},{12,76},{16,80},{20,84},{24,88},{28,92},{32,9... | collective-permute-start | bytes 491528 | tf_op jit(solution)/shard_map/ppermute | solution.py:316
  184.5 29.2 %collective-permute-start.18 = (bf16[128,640]{1,0:T(8,128)(2,1)}, bf16[128,640]{1,0:T(8,128)(2,1)S(1)}, u32[]{:S(2)}, u32[]{:S(2)}) collective-permute-start(bf16[128,640]{1,0:T(8,128)(2,1)} %copy-done.21), channel_id=1, source_target_pairs={{0,68},{4,64},{8,76},{12,72},{16,84},{20,80},{24,92},{28,88},{32,1... | collective-permute-start | bytes 491528 | tf_op jit(solution)/shard_map/ppermute | solution.py:316
  186.3 28.0 %collective-permute-start.19 = (bf16[128,640]{1,0:T(8,128)(2,1)}, bf16[128,640]{1,0:T(8,128)(2,1)S(1)}, u32[]{:S(2)}, u32[]{:S(2)}) collective-permute-start(bf16[128,640]{1,0:T(8,128)(2,1)} %copy-done.20), channel_id=1, source_target_pairs={{0,128},{4,132},{8,136},{12,140},{16,144},{20,148},{24,152},{28,15... | collective-permute-start | bytes 491528 | tf_op jit(solution)/shard_map/ppermute | solution.py:316
  188.5 26.5 %collective-permute-start.20 = (bf16[128,640]{1,0:T(8,128)(2,1)}, bf16[128,640]{1,0:T(8,128)(2,1)}, u32[]{:S(2)}, u32[]{:S(2)}) collective-permute-start(bf16[128,640]{1,0:T(8,128)(2,1)} %copy-done.19), channel_id=1, source_target_pairs={{0,132},{4,128},{8,140},{12,136},{16,148},{20,144},{24,156},{28,15... | collective-permute-start | bytes 491528 | tf_op jit(solution)/shard_map/ppermute | solution.py:316
  189.1 25.9 %collective-permute-start.21 = (bf16[128,640]{1,0:T(8,128)(2,1)}, bf16[128,640]{1,0:T(8,128)(2,1)}, u32[]{:S(2)}, u32[]{:S(2)}) collective-permute-start(bf16[128,640]{1,0:T(8,128)(2,1)} %copy-done.18), channel_id=1, source_target_pairs={{0,192},{4,196},{8,200},{12,204},{16,208},{20,212},{24,216},{28,22... | collective-permute-start | bytes 491528 | tf_op jit(solution)/shard_map/ppermute | solution.py:316
  194.0 21.0 %collective-permute-start.22 = (bf16[128,640]{1,0:T(8,128)(2,1)}, bf16[128,640]{1,0:T(8,128)(2,1)}, u32[]{:S(2)}, u32[]{:S(2)}) collective-permute-start(bf16[128,640]{1,0:T(8,128)(2,1)} %copy-done.17), channel_id=1, source_target_pairs={{0,196},{4,192},{8,204},{12,200},{16,212},{20,208},{24,220},{28,21... | collective-permute-start | bytes 491528 | tf_op jit(solution)/shard_map/ppermute | solution.py:316
  223.8 9.1 %collective-permute-start.23 = (bf16[128,1024]{1,0:T(8,128)(2,1)}, bf16[128,1024]{1,0:T(8,128)(2,1)S(1)}, u32[]{:S(2)}, u32[]{:S(2)}) collective-permute-start(bf16[128,1024]{1,0:T(8,128)(2,1)} %get-tuple-element.31), channel_id=1, source_target_pairs={{0,1},{1,2},{2,3},{3,0},{4,5},{5,6},{6,7},{7,4},{8,9},{9,10},{10,1... | collective-permute-start | bytes 786440 | tf_op jit(solution)/shard_map/ppermute | solution.py:302
  225.1 14.3 %collective-permute-start.24 = (bf16[128,1024]{1,0:T(8,128)(2,1)}, bf16[128,1024]{1,0:T(8,128)(2,1)S(1)}, u32[]{:S(2)}, u32[]{:S(2)}) collective-permute-start(bf16[128,1024]{1,0:T(8,128)(2,1)} %get-tuple-element.32), channel_id=1, source_target_pairs={{0,2},{1,3},{2,0},{3,1},{4,6},{5,7},{6,4},{7,5},{8,10},{9,11},{10,... | collective-permute-start | bytes 786440 | tf_op jit(solution)/shard_map/ppermute | solution.py:302
  227.4 12.0 %collective-permute-start.25 = (bf16[128,1024]{1,0:T(8,128)(2,1)}, bf16[128,1024]{1,0:T(8,128)(2,1)}, u32[]{:S(2)}, u32[]{:S(2)}) collective-permute-start(bf16[128,1024]{1,0:T(8,128)(2,1)} %get-tuple-element.33), channel_id=1, source_target_pairs={{0,3},{1,0},{2,1},{3,2},{4,7},{5,4},{6,5},{7,6},{8,11},{9,8},{10,9... | collective-permute-start | bytes 786440 | tf_op jit(solution)/shard_map/ppermute | solution.py:302
  (30 other events, 74.9 us)
Sparse Core Ops, SparseCore 0:
  10.7 106.7 all-gather.2
  120.3 93.2 all-gather.4

commit v2 on v1

v2 whole, which is shorter than its diff:
```python
import functools
import math

import jax
import jax.numpy as jnp
from jax import lax
from jax.experimental import pallas as pl
from jax.experimental.pallas import tpu as pltpu
from jax.sharding import Mesh, PartitionSpec as P

HD = 80
CAP = 64
LROWS = 160
NY, NZ, NC = 4, 8, 2
EPSILON = 1e-06
BF = jnp.bfloat16
F32 = jnp.float32


def dot_tn(lhs, rhs):
    return lax.dot_general(lhs, rhs, (((0,), (0,)), ((), ())), preferred_element_type=F32)


def dot_nt(lhs, rhs):
    return lax.dot_general(lhs, rhs, (((1,), (1,)), ((), ())), preferred_element_type=F32)


def dot_nn(lhs, rhs):
    return jnp.dot(lhs, rhs, preferred_element_type=F32)


def params(mib=60):
    return pltpu.CompilerParams(vmem_limit_bytes=mib * 1024 * 1024)


def cost(microseconds):
    return pl.CostEstimate(
        flops=int(microseconds * 3.3e9), bytes_accessed=2**20, transcendentals=0
    )


def whole(shape):
    return pl.BlockSpec(shape, lambda *_: (0,) * len(shape))


def attention_kernel(
    member_ref, a0, a1, a2, a3, gain, w_qkv, b_qkv, w_proj, key_tag, p0, p1, p2, p3, normed, context
):
    width, rows = normed.shape
    cols = width // 4
    heads = cols // HD
    member = member_ref[0]
    pieces = [ref[...].astype(F32) for ref in (a0, a1, a2, a3)]
    square = sum(jnp.sum(piece * piece, axis=0, keepdims=True) for piece in pieces)
    inverse = lax.rsqrt(square * (1.0 / width) + EPSILON)
    for shift, piece in enumerate(pieces):
        owner = lax.rem(member - shift + 4, 4)
        span = pl.ds(pl.multiple_of(owner * cols, 64), cols)
        normed[span, :] = (piece * inverse * gain[span, :]).astype(BF)
    qkv = (dot_nn(w_qkv[...], normed[...]) + b_qkv[...]).astype(BF)
    query_image = lax.broadcasted_iota(jnp.int32, (rows, rows), 1) // CAP + pl.program_id(0) * (
        rows // CAP
    )
    allowed = key_tag[...] == query_image
    for head in range(heads):
        query = qkv[head * HD : (head + 1) * HD]
        key = qkv[cols + head * HD : cols + (head + 1) * HD]
        value = qkv[2 * cols + head * HD : 2 * cols + (head + 1) * HD]
        scores = dot_tn(key, query) * (1.0 / math.sqrt(HD))
        scores = jnp.where(allowed, scores, -1e30)
        scores = jnp.exp(scores - jnp.max(scores, axis=0, keepdims=True))
        weights = (scores / jnp.sum(scores, axis=0, keepdims=True)).astype(BF)
        context[head * HD : (head + 1) * HD, :] = dot_nn(value, weights).astype(BF)
    for shift, out in enumerate((p0, p1, p2, p3)):
        owner = lax.rem(member + shift, 4)
        span = pl.ds(pl.multiple_of(owner * cols, 64), cols)
        out[...] = dot_nn(w_proj[span, :], context[...]).astype(BF)


def attention(member, pieces, gain, w_qkv, b_qkv, w_proj, key_tag, step_rows=256):
    cols, rows = pieces[0].shape
    width = cols * 4
    piece_spec = pl.BlockSpec((cols, step_rows), lambda i, *_: (0, i))
    return pl.pallas_call(
        attention_kernel,
        grid_spec=pltpu.PrefetchScalarGridSpec(
            num_scalar_prefetch=1,
            grid=(rows // step_rows,),
            in_specs=[piece_spec] * 4
            + [
                whole((width, 1)),
                whole((3 * cols, width)),
                whole((3 * cols, 1)),
                whole((width, cols)),
                pl.BlockSpec((step_rows, 1), lambda i, *_: (i, 0)),
            ],
            out_specs=[piece_spec] * 4,
            scratch_shapes=[
                pltpu.VMEM((width, step_rows), BF),
                pltpu.VMEM((cols, step_rows), BF),
            ],
        ),
        out_shape=[jax.ShapeDtypeStruct((cols, rows), BF)] * 4,
        compiler_params=params(20),
        cost_estimate=cost(9),
        name="attention",
    )(member, *pieces, gain, w_qkv, b_qkv, w_proj, key_tag)


def expand_kernel(at_ref, e0, e1, e2, e3, gain, weight, bias, *refs):
    out, normed, turned, total = refs[-4:]
    width, rows = normed.shape
    cols = width // 4
    merged = rows // 4
    shift_y = pl.program_id(0)
    member = at_ref[0]

    @pl.when(shift_y == 0)
    def _():
        pieces = [ref[...].astype(F32) for ref in (e0, e1, e2, e3)]
        square = sum(jnp.sum(piece * piece, axis=0, keepdims=True) for piece in pieces)
        inverse = lax.rsqrt(square * (1.0 / width) + EPSILON)
        for shift, piece in enumerate(pieces):
            owner = lax.rem(member - shift + 4, 4)
            span = pl.ds(pl.multiple_of(owner * cols, 64), cols)
            normed[span, :] = (piece * inverse * gain[span, :]).astype(BF)
        into = lax.broadcasted_iota(jnp.int32, (rows, rows), 0)
        picks = lax.broadcasted_iota(jnp.int32, (rows, rows), 1) == 4 * (
            into % merged
        ) + into // merged
        turned[...] = dot_nt(picks.astype(F32).astype(BF), normed[...]).astype(BF)
        total[...] = jnp.zeros_like(total)

    position = lax.rem(at_ref[1] - shift_y + NY, NY)
    span = pl.ds(pl.multiple_of(position * merged, 128), merged)
    total[...] += dot_nn(turned[span, :], weight[...].reshape(width, total.shape[1]))

    @pl.when(shift_y == NY - 1)
    def _():
        value = total[...] + bias[...]
        out[...] = (0.5 * value * (1.0 + lax.erf(value * (1.0 / math.sqrt(2.0))))).astype(BF)


def expand(at, pieces, gain, weight, bias, after):
    cols, rows = pieces[0].shape
    width = cols * 4
    chunk, hidden = width // (NZ * NC), weight.shape[4]
    return pl.pallas_call(
        expand_kernel,
        grid_spec=pltpu.PrefetchScalarGridSpec(
            num_scalar_prefetch=1,
            grid=(NY,),
            in_specs=[whole((cols, rows))] * 4
            + [
                whole((width, 1)),
                pl.BlockSpec((NZ, NC, 1, chunk, hidden), lambda i, *_: (0, 0, i, 0, 0)),
                whole((1, hidden)),
            ]
            + [pl.BlockSpec(memory_space=pl.ANY)] * len(after),
            out_specs=whole((rows // 4, hidden)),
            scratch_shapes=[
                pltpu.VMEM((width, rows), BF),
                pltpu.VMEM((rows, width), BF),
                pltpu.VMEM((rows // 4, hidden), F32),
            ],
        ),
        out_shape=jax.ShapeDtypeStruct((rows // 4, hidden), BF),
        compiler_params=params(),
        cost_estimate=cost(6),
        name="expand",
    )(at, *pieces, gain, weight, bias, *after)


def route_kernel(*refs):
    source, blocks, outs, held = refs[0], refs[1:9], refs[-9:-1], refs[-1]
    rows = blocks[0].shape[0]
    for at, block in enumerate(blocks):
        held[at * rows : (at + 1) * rows, :] = block[...]
    for at, out in enumerate(outs):
        wanted = source[at * rows : (at + 1) * rows, :]
        picks = lax.broadcasted_iota(jnp.int32, (rows, held.shape[0]), 1) == wanted
        out[...] = dot_nn(picks.astype(F32).astype(BF), held[...]).astype(BF)


def route(source, blocks):
    rows, hidden = blocks[0].shape
    return pl.pallas_call(
        route_kernel,
        out_shape=[jax.ShapeDtypeStruct((rows, hidden), BF)] * 8,
        scratch_shapes=[pltpu.VMEM((8 * rows, hidden), BF)],
        compiler_params=params(),
        cost_estimate=cost(4),
        name="route",
    )(source, *blocks)


def output_kernel(at_ref, *refs):
    blocks, weight, outs, held = refs[:8], refs[8], refs[9:13], refs[13]
    part = pl.program_id(0)

    @pl.when(part == 0)
    def _():
        held[...] = sum(block[...].astype(F32) for block in blocks).astype(BF)

    flat = weight[...].reshape(outs[0].shape[1], held.shape[1])
    result = dot_nt(held[...], flat).astype(BF)
    for at, out in enumerate(outs):

        @pl.when(part == at)
        def _(out=out):
            out[...] = result


def output_map(at, blocks, weight, chunk):
    rows, hidden = blocks[0].shape
    cols = NZ * NC * chunk
    weight = weight.reshape(NZ * NC, weight.shape[1] // chunk, chunk, hidden)
    return pl.pallas_call(
        output_kernel,
        grid_spec=pltpu.PrefetchScalarGridSpec(
            num_scalar_prefetch=1,
            grid=(4,),
            in_specs=[whole((rows, hidden))] * 8
            + [
                pl.BlockSpec(
                    (NZ * NC, 1, chunk, hidden),
                    lambda i, at: (0, lax.rem(at[1] - at[0] - i + 8, 4), 0, 0),
                )
            ],
            out_specs=[whole((rows, cols))] * 4,
            scratch_shapes=[pltpu.VMEM((rows, hidden), BF)],
        ),
        out_shape=[jax.ShapeDtypeStruct((rows, cols), BF)] * 4,
        compiler_params=params(),
        cost_estimate=cost(6),
        name="output_map",
    )(at, *blocks, weight)


def place_kernel(p0, p1, p2, p3, bias, source, out):
    total = sum(ref[...].astype(F32) for ref in (p0, p1, p2, p3)) + bias[...]
    rows = p0.shape[0]
    picks = lax.broadcasted_iota(jnp.int32, (out.shape[0], rows), 1) == source[...]
    out[...] = dot_nn(picks.astype(F32).astype(BF), total.astype(BF)).astype(BF)


def place(parts, bias, source):
    cols = parts[0].shape[1]
    return pl.pallas_call(
        place_kernel,
        out_shape=jax.ShapeDtypeStruct((source.shape[0], cols), BF),
        compiler_params=params(),
        cost_estimate=cost(3),
        name="place",
    )(*parts, bias, source)


def bundle_kernel(rows_ref, *refs):
    out = refs[-1]
    shards = refs[:NY]
    chunk, width = shards[0].shape
    for at, shard in enumerate(shards):
        out[at * chunk : (at + 1) * chunk, :] = shard[...]
    blocks = width // CAP
    depth = rows_ref.shape[0] // blocks
    for image in range(rows_ref.shape[1] // CAP):
        parts = [
            rows_ref[at * depth : (at + 1) * depth, image * CAP : (image + 1) * CAP]
            for at in range(blocks)
        ]
        first = NY * chunk + image * depth
        out[first : first + depth, :] = jnp.concatenate(parts, axis=1)


def bundle(rows_t, shards):
    chunk, width = shards[0].shape
    rows = NY * chunk + rows_t.size // width
    return pl.pallas_call(
        bundle_kernel,
        out_shape=jax.ShapeDtypeStruct((rows, width), BF),
        compiler_params=params(),
        cost_estimate=cost(3),
        name="bundle",
    )(rows_t, *shards)


def spread_kernel(source, bundles, *refs):
    outs, sems = refs[-NY - 1 : -1], refs[-1]
    images, depth, _ = outs[0].shape
    first = bundles.shape[1] - images * depth

    def copy(out, group, slot):
        at = jnp.maximum(source[group * images + slot], 0)
        row = pl.multiple_of(first + at % images * depth, depth)
        return pltpu.make_async_copy(
            bundles.at[at // images, pl.ds(row, depth), :],
            out.at[slot],
            sems.at[group * images + slot],
        )

    for group, out in enumerate(outs):
        out[...] = jnp.zeros_like(out)

        @pl.loop(0, images)
        def _(slot, group=group, out=out):
            @pl.when(source[group * images + slot] >= 0)
            def _():
                copy(out, group, slot).start()

    for group, out in enumerate(outs):

        @pl.loop(0, images)
        def _(slot, group=group, out=out):
            @pl.when(source[group * images + slot] >= 0)
            def _():
                copy(out, group, slot).wait()


def spread(source, bundles, depth, after):
    slots = source.shape[0]
    anywhere = pl.BlockSpec(memory_space=pl.ANY)
    return pl.pallas_call(
        spread_kernel,
        in_specs=[pl.BlockSpec(memory_space=pltpu.SMEM), anywhere] + [anywhere] * len(after),
        out_shape=[jax.ShapeDtypeStruct((slots // NY, depth, bundles.shape[2]), BF)] * NY,
        scratch_shapes=[pltpu.SemaphoreType.DMA((slots,))],
        compiler_params=params(),
        cost_estimate=cost(4),
        name="spread",
    )(source, bundles, *after)


def unpack_kernel(*refs):
    groups, out = refs[:-1], refs[-1]
    count, depth, width = groups[0].shape
    for at in range(count // 2):
        first, second = (
            sum(group[image].astype(F32) for group in groups).astype(BF)
            for image in (2 * at, 2 * at + 1)
        )
        for block in range(width // CAP):
            span = slice(block * CAP, (block + 1) * CAP)
            out[block * depth : (block + 1) * depth, 2 * CAP * at : 2 * CAP * (at + 1)] = (
                jnp.concatenate([first[:, span], second[:, span]], axis=1)
            )


def unpack(groups):
    count, depth, width = groups[0].shape
    return pl.pallas_call(
        unpack_kernel,
        out_shape=jax.ShapeDtypeStruct((depth * width // CAP, count * CAP), BF),
        compiler_params=params(),
        cost_estimate=cost(2),
        name="unpack",
    )(*groups)


def axis_shift(values, axis, size, shift):
    return lax.ppermute(values, axis, [(i, (i + shift) % size) for i in range(size)])


def tensor_shift(values, shift):
    return axis_shift(values, "tensor", 4, shift)


def z_shift(values, shift):
    return axis_shift(values, "z", NZ, shift)


def yc_shift(values, dy, dc):
    pairs = [
        (y * NC + c, (y + dy) % NY * NC + (c + dc) % NC) for y in range(NY) for c in range(NC)
    ]
    return lax.ppermute(values, ("y", "c"), pairs)


def stack_kernel(*refs):
    for at in range(NY):
        refs[-1][at] = refs[at][...]


def stack(values):
    return pl.pallas_call(
        stack_kernel,
        out_shape=jax.ShapeDtypeStruct((NY, *values[0].shape), BF),
        compiler_params=params(),
        cost_estimate=cost(1),
        name="stack",
    )(*values)


def hold_kernel(value, _, out):
    out[...] = value[...]


def hold(value, after):
    in_vmem = pl.BlockSpec(memory_space=pltpu.VMEM)
    return pl.pallas_call(
        hold_kernel,
        in_specs=[in_vmem, pl.BlockSpec(memory_space=pl.ANY)],
        out_shape=jax.ShapeDtypeStruct(value.shape, value.dtype),
        compiler_params=params(),
        cost_estimate=cost(1),
        name="hold",
    )(value, after)


def ring_near(values):
    return {shift: z_shift(values, shift) for shift in (1, -1, 2, -2)}


def ring_far(near):
    return {3: z_shift(near[2], 1), -3: z_shift(near[-2], -1), 4: z_shift(near[2], 2)}


def along_y(shard):
    return [shard] + [axis_shift(shard, "y", NY, shift) for shift in (1, 2, 3)]


def gather_zc(values):
    return lax.all_gather(values, ("z", "c"), axis=0)


def per_device(
    patches,
    counts,
    source_slot,
    target_slot,
    lang_start,
    window_order,
    norm_gain,
    qkv_weight,
    qkv_bias,
    proj_weight,
    proj_bias,
    merge_gain,
    expand_weight,
    expand_bias,
    output_weight,
    output_bias,
):
    at_y, at_z, at_c = lax.axis_index("y"), lax.axis_index("z"), lax.axis_index("c")
    dp_index = (at_y * NZ + at_z) * NC + at_c
    member = lax.axis_index("tensor")
    rows, cols = patches.shape
    images = rows // CAP
    depth = CAP // 4
    width = cols * 4
    at = jnp.stack([member, at_y]).astype(jnp.int32)

    own = patches.T
    pieces = [own] + [tensor_shift(own, shift) for shift in (1, 2, 3)]
    expand_full = gather_zc(stack(along_y(expand_weight)))
    expand_full = expand_full.reshape(NZ, NC, *expand_full.shape[1:])

    slot_ids = dp_index * images + jnp.arange(images, dtype=jnp.int32)
    held = source_slot[None, :] == slot_ids[:, None]
    live_count = jnp.sum(jnp.where(held, counts[None, :], 0), axis=1)
    row_ids = jnp.arange(CAP, dtype=jnp.int32)
    live = row_ids[None, :] < live_count[:, None]
    image_ids = jnp.arange(images, dtype=jnp.int32)
    key_tag = jnp.where(live, image_ids[:, None], -1).reshape(rows, 1)
    live_row = live.reshape(1, rows)

    def plane(table):
        tail = table.shape[1:]
        table = table.reshape(NY, NZ, NC, images, *tail)
        table = lax.dynamic_index_in_dim(table, at_z, 1, keepdims=False)
        table = lax.dynamic_slice_in_dim(jnp.concatenate([table, table], 0), at_y, NY, 0)
        return lax.dynamic_slice_in_dim(jnp.concatenate([table, table], 1), at_c, NC, 1)

    near_slots = ((at_y + jnp.arange(NY)[:, None]) % NY * NZ + at_z) * NC + at_c
    near_slots = (near_slots * images + image_ids).reshape(-1, 1).astype(jnp.int32)
    bound = target_slot[None, :] == near_slots
    bound_source = jnp.sum(jnp.where(bound, source_slot[None, :], 0), axis=1)
    column = NZ * NC * images
    spread_source = jnp.where(bound_source // column == at_y, bound_source % column, -1)

    plane_source = plane(source_slot)
    plane_rank = plane_source // images
    here = jnp.logical_and(plane_rank // (NZ * NC) == at_y, plane_rank % NC == at_c)
    step = (at_z - plane_rank // NC % NZ + NZ) % NZ
    base = (step * images + plane_source % images) * depth
    route_source = jnp.where(here[..., None], base[..., None] + plane(window_order), -1)
    route_source = route_source.reshape(NY * NC * images * depth, 1)

    own_start = (
        lax.dynamic_slice_in_dim(lang_start, dp_index * images, images, 0) - dp_index * LROWS
    )
    own_used = lax.dynamic_slice_in_dim(counts, dp_index * images, images, 0) // 4
    lang_rows = jnp.arange(LROWS, dtype=jnp.int32)[:, None]
    inside = jnp.logical_and(
        lang_rows >= own_start[None, :], lang_rows < own_start[None, :] + own_used[None, :]
    )
    place_source = (
        jnp.sum(
            jnp.where(inside, image_ids[None, :] * depth + lang_rows - own_start[None, :] + 1, 0),
            axis=1,
            keepdims=True,
        )
        - 1
    )

    parts = attention(
        at,
        pieces,
        norm_gain.reshape(width, 1),
        qkv_weight.transpose(1, 2, 0).reshape(3 * cols, width),
        qkv_bias.reshape(3 * cols, 1),
        proj_weight.T,
        key_tag,
    )
    arrived = [tensor_shift(parts[shift], shift) for shift in (1, 2, 3)]
    summed = sum(part.astype(F32) for part in [parts[0]] + arrived)
    own_bias = lax.dynamic_slice_in_dim(proj_bias, member * cols, cols, 0)
    hidden = own.astype(F32) + summed + own_bias[:, None]
    encoded_here = jnp.where(live_row, hidden, 0.0).astype(BF)

    encoded_pieces = [encoded_here] + [tensor_shift(encoded_here, shift) for shift in (1, 2, 3)]
    output_shards = along_y(hold(output_weight.T, parts[0]))
    bundles = gather_zc(bundle(encoded_here, output_shards))
    expanded = expand(
        at,
        encoded_pieces,
        merge_gain.reshape(width, 1),
        expand_full,
        expand_bias.reshape(1, -1),
        [],
    )
    near = ring_near(expanded)
    ring = {0: expanded, **near, **ring_far(near)}
    ring = [ring[shift] if shift in ring else ring[shift - NZ] for shift in range(NZ)]
    routed = route(route_source, ring)
    blocks = [routed[0]]
    for slot in range(1, NY * NC):
        blocks.append(yc_shift(routed[slot], slot // NC, slot % NC))
    packed_depth = rows * cols // images // output_weight.shape[0]
    leaving = spread(spread_source, bundles, packed_depth, blocks[1:])
    landed = [leaving[0]] + [axis_shift(leaving[k], "y", NY, k) for k in (1, 2, 3)]
    out_parts = output_map(at, blocks, bundles, output_weight.shape[1])
    out_arrived = [tensor_shift(out_parts[shift], shift) for shift in (1, 2, 3)]
    merged = place([out_parts[0]] + out_arrived, output_bias.reshape(1, -1), place_source)
    encoded = unpack(landed).T
    return (encoded, merged)


def solution(mesh):
    fine_mesh = Mesh(mesh.devices.reshape(NY, NZ, NC, 4), ("y", "z", "c", "tensor"))
    dp = ("y", "z", "c")
    in_specs = (
        P(dp, "tensor"),
        P(),
        P(),
        P(),
        P(),
        P(),
        P(),
        P(None, None, "tensor"),
        P(None, "tensor"),
        P("tensor", None),
        P(),
        P(),
        P(dp, "tensor"),
        P("tensor"),
        P("tensor", dp),
        P("tensor"),
    )
    out_specs = (P(dp, "tensor"), P(dp, "tensor"))
    return jax.shard_map(
        per_device, mesh=fine_mesh, in_specs=in_specs, out_specs=out_specs, check_vma=False
    )
```

time: 251 us -> 214 us (0.85)
  waiting for transfers between devices: 123 us -> 83 us
  local copies, waits for them, and re-layouts: 32.7 us -> 15.4 us
  Pallas kernels: 25.4 us -> 41.7 us
  starting transfers between devices: 50.7 us -> 54.4 us
    all_gather x2, waiting for transfers between devices: 39.4 us -> 0.01 us  [gather_zc(): return lax.all_gather(values, ('z', 'c'), axis=0)]
    unnamed x68 -> x90, local copies, waits for them, and re-layouts: 27.2 us -> 10 us
    ppermute x26 -> x35, starting transfers between devices: 37.3 us -> 54.3 us  [the longest x28 44.2 us: axis_shift(): lax.ppermute(values, axis, [(i, (i + shift) % size) for i in range(size)])]
    all_to_all x1 -> x0, starting transfers between devices: 13.3 us -> none  [per_device(): lax.all_to_all(leaving, 'dp', split_axis=0, concat_axis=0, tiled=True)]
    pallas_call x2 -> x5, Pallas kernels: 3.32 us -> 11.1 us  [the longest x1 3.41 us: spread(): pl.pallas_call(spread_kernel, in_specs=[pl.BlockSpec(memory_space=pltpu.S...]
    pallas_call x1, Pallas kernels: 4.16 us -> 7.94 us  [expand(): pl.pallas_call(expand_kernel, grid_spec=pltpu.PrefetchScalarGridSpec(num_...]
    ppermute x26 -> x35, waiting for transfers between devices: 81.9 us -> 83 us  [the longest x28 72.9 us: axis_shift(): lax.ppermute(values, axis, [(i, (i + shift) % size) for i in range(size)])]
  transfers between devices with their start and end apart: 29 -> 37, of which waited for: 14 -> 20; matrix products, arithmetic and copies ran while one was open for 4% -> 4% of each run, Pallas kernels for 9% -> 15%
where the time goes in v2:
time: 214 us; the launch traced here: 212 us
  waiting for transfers between devices  83 us (39%)
  starting transfers between devices  54.4 us (25%)
  Pallas kernels  41.7 us (19%)
  local copies, waits for them, and re-layouts  15.4 us (7%)
  between operations  14.5 us (7%)
  other arithmetic  3.31 us (2%)
    ppermute x28, waiting for transfers between devices, axis_shift(): lax.ppermute(values, axis, [(i, (i + shift) % size) for i in range(size)])  72.9 us
    ppermute x28, starting transfers between devices, axis_shift(): lax.ppermute(values, axis, [(i, (i + shift) % size) for i in range(size)])  44.2 us
    ppermute x7, waiting for transfers between devices, yc_shift(): return lax.ppermute(values, ('y', 'c'), pairs)  10.1 us
    ppermute x7, starting transfers between devices, yc_shift(): return lax.ppermute(values, ('y', 'c'), pairs)  10.1 us
    unnamed x90, local copies, waits for them, and re-layouts  10 us
    pallas_call x1, Pallas kernels, attention(): pl.pallas_call(attention_kernel, grid_spec=pltpu.PrefetchScalarGridSpec(n...  9.49 us
    pallas_call x1, Pallas kernels, expand(): pl.pallas_call(expand_kernel, grid_spec=pltpu.PrefetchScalarGridSpec(num_...  7.94 us
    pallas_call x1, Pallas kernels, output_map(): pl.pallas_call(output_kernel, grid_spec=pltpu.PrefetchScalarGridSpec(num_...  6.76 us
  transfers between devices with their start and end apart: 37, of which 20 were waited for; matrix products, arithmetic and copies ran while one was open for 4% of the time, Pallas kernels for 15%

profile of v2, /device:TPU:1, one launch (start us, length us, event | category | flops | bytes accessed | tf_op | source)
XLA Modules:
  0.0 212.2 jit_solution(6788245232927568501)
XLA Ops:
  7.3 2.2 %collective-permute-start.12 = (bf16[80,640]{1,0:T(8,128)(2,1)}, bf16[80,640]{1,0:T(8,128)(2,1)S(1)}, u32[]{:S(2)}, u32[]{:S(2)}) collective-permute-start(bf16[80,640]{1,0:T(8,128)(2,1)} %refs_0_.1), channel_id=1, source_target_pairs={{0,64},{64,128},{128,192},{192,0},{1,65},{65,129},{129,193},{193,1... | collective-permute-start | bytes 307208 | tf_op jit(solution)/shard_map/ppermute | solution.py:360
  9.5 2.6 %collective-permute-start.13 = (bf16[80,640]{1,0:T(8,128)(2,1)}, bf16[80,640]{1,0:T(8,128)(2,1)S(1)}, u32[]{:S(2)}, u32[]{:S(2)}) collective-permute-start(bf16[80,640]{1,0:T(8,128)(2,1)} %refs_0_.1), channel_id=1, source_target_pairs={{0,128},{64,192},{128,0},{192,64},{1,129},{65,193},{129,1},{193,65... | collective-permute-start | bytes 307208 | tf_op jit(solution)/shard_map/ppermute | solution.py:360
  13.2 3.3 %collective-permute-done.13.refs_2_ = bf16[80,640]{1,0:T(8,128)(2,1)S(1)} collective-permute-done((bf16[80,640]{1,0:T(8,128)(2,1)}, bf16[80,640]{1,0:T(8,128)(2,1)S(1)}, u32[]{:S(2)}, u32[]{:S(2)}) %collective-permute-start.13) | collective-permute-done | bytes 102432 | tf_op jit(solution)/shard_map/ppermute | solution.py:360
  21.0 2.5 %collective-permute-start.1 = (bf16[320,512]{1,0:T(8,128)(2,1)S(1)}, bf16[320,512]{1,0:T(8,128)(2,1)S(1)}, u32[]{:S(2)}, u32[]{:S(2)}) collective-permute-start(bf16[320,512]{1,0:T(8,128)(2,1)S(1)} %bitcast.24), channel_id=1, source_target_pairs={{0,2},{1,3},{2,0},{3,1},{4,6},{5,7},{6,4},{7,5},{8,10},{9,11},{10,... | collective-permute-start | bytes 983048 | tf_op jit(solution)/shard_map/ppermute | solution.py:360
  28.1 8.3 %collective-permute-done.1.a2 = bf16[320,512]{1,0:T(8,128)(2,1)S(1)} collective-permute-done((bf16[320,512]{1,0:T(8,128)(2,1)S(1)}, bf16[320,512]{1,0:T(8,128)(2,1)S(1)}, u32[]{:S(2)}, u32[]{:S(2)}) %collective-permute-start.1) | collective-permute-done | bytes 327712 | tf_op jit(solution)/shard_map/ppermute | solution.py:360
  38.7 9.5 %attention.1 = (bf16[320,512]{1,0:T(8,128)(2,1)S(1)}, bf16[320,512]{1,0:T(8,128)(2,1)}, bf16[320,512]{1,0:T(8,128)(2,1)}, bf16[320,512]{1,0:T(8,128)(2,1)}) custom-call(s32[2]{0:T(128)S(1)} %pad_add_fusion.member_ref.at_ref, bf16[320,512]{1,0:T(8,128)(2,1)S(1)} %bitcast.26, bf16[320,512]{1,0:T(8,128)(2,1)S(1)} %collective-permute-done.a1, ...), custom_call_target="tpu_custom_call" | custom-call | flops 29699999744 | bytes 1048576 | tf_op jit(solution)/shard_map/attention/pallas_call | solution.py:84
  48.9 2.1 collective-permute-start.3
  51.0 2.6 %collective-permute-start.4 = (bf16[320,512]{1,0:T(8,128)(2,1)}, bf16[320,512]{1,0:T(8,128)(2,1)S(1)}, u32[]{:S(2)}, u32[]{:S(2)}) collective-permute-start(bf16[320,512]{1,0:T(8,128)(2,1)} %get-tuple-element.24), channel_id=1, source_target_pairs={{0,2},{1,3},{2,0},{3,1},{4,6},{5,7},{6,4},{7,5},{8,10},{9,11},{10,... | collective-permute-start | bytes 983048 | tf_op jit(solution)/shard_map/ppermute | solution.py:360
  56.1 2.2 %collective-permute-start.7 = (bf16[64,640]{1,0:T(8,128)(2,1)}, bf16[64,640]{1,0:T(8,128)(2,1)S(1)}, u32[]{:S(2)}, u32[]{:S(2)}) collective-permute-start(bf16[64,640]{1,0:T(8,128)(2,1)} %hold.1.refs_0_), channel_id=1, source_target_pairs={{0,128},{64,192},{128,0},{192,64},{1,129},{65,193},{129,1},{193,65... | collective-permute-start | bytes 245768 | tf_op jit(solution)/shard_map/ppermute | solution.py:360
  60.0 7.9 %collective-permute-done.4 = bf16[320,512]{1,0:T(8,128)(2,1)S(1)} collective-permute-done((bf16[320,512]{1,0:T(8,128)(2,1)}, bf16[320,512]{1,0:T(8,128)(2,1)S(1)}, u32[]{:S(2)}, u32[]{:S(2)}) %collective-permute-start.4) | collective-permute-done | bytes 327712 | tf_op jit(solution)/shard_map/ppermute | solution.py:360
  70.2 2.1 bundle.1
  75.8 2.8 %collective-permute-start.11 = (bf16[320,512]{1,0:T(8,128)(2,1)S(1)}, bf16[320,512]{1,0:T(8,128)(2,1)S(1)}, u32[]{:S(2)}, u32[]{:S(2)}) collective-permute-start(bf16[320,512]{1,0:T(8,128)(2,1)S(1)} %copy-done.6), channel_id=1, source_target_pairs={{0,3},{1,0},{2,1},{3,2},{4,7},{5,4},{6,5},{7,6},{8,11},{9,8},{10,9... | collective-permute-start | bytes 983048 | tf_op jit(solution)/shard_map/ppermute | solution.py:360
  78.6 5.0 %collective-permute-done.10.e2 = bf16[320,512]{1,0:T(8,128)(2,1)S(1)} collective-permute-done((bf16[320,512]{1,0:T(8,128)(2,1)S(1)}, bf16[320,512]{1,0:T(8,128)(2,1)S(1)}, u32[]{:S(2)}, u32[]{:S(2)}) %collective-permute-start.10) | collective-permute-done | bytes 327712 | tf_op jit(solution)/shard_map/ppermute | solution.py:360
  83.6 9.2 %collective-permute-done.11.e3 = bf16[320,512]{1,0:T(8,128)(2,1)S(1)} collective-permute-done((bf16[320,512]{1,0:T(8,128)(2,1)S(1)}, bf16[320,512]{1,0:T(8,128)(2,1)S(1)}, u32[]{:S(2)}, u32[]{:S(2)}) %collective-permute-start.11) | collective-permute-done | bytes 327712 | tf_op jit(solution)/shard_map/ppermute | solution.py:360
  93.6 7.9 %expand.1.refs_1_ = bf16[128,640]{1,0:T(8,128)(2,1)} custom-call(s32[2]{0:T(128)} %copy-done.4, bf16[320,512]{1,0:T(8,128)(2,1)} %select_convert_fusion.rows_ref.e0, bf16[320,512]{1,0:T(8,128)(2,1)} %copy-done.20, bf16[320,512]{1,0:T(8,128)(2,1)} %copy-done.17, bf16[320,512]{1,0:T(8,128)(2,1)} %copy-done.18, f32[1280,1]{1,0:T(8,128)} %reshape.183.gain, ...), custom_call_target="tpu_custom_call" | custom-call | flops 19800000512 | bytes 1048576 | tf_op jit(solution)/shard_map/expand/pallas_call | solution.py:148
  101.5 3.2 %collective-permute-start.16 = (bf16[128,640]{1,0:T(8,128)(2,1)}, bf16[128,640]{1,0:T(8,128)(2,1)S(1)}, u32[]{:S(2)}, u32[]{:S(2)}) collective-permute-start(bf16[128,640]{1,0:T(8,128)(2,1)} %expand.1.refs_1_), channel_id=1, source_target_pairs={{0,16},{8,24},{16,32},{24,40},{32,48},{40,56},{48,0},{56,8},{1,17}... | collective-permute-start | bytes 491528 | tf_op jit(solution)/shard_map/ppermute | solution.py:360
  104.7 3.0 %collective-permute-start.19 = (bf16[128,640]{1,0:T(8,128)(2,1)}, bf16[128,640]{1,0:T(8,128)(2,1)S(1)}, u32[]{:S(2)}, u32[]{:S(2)}) collective-permute-start(bf16[128,640]{1,0:T(8,128)(2,1)} %expand.1.refs_1_), channel_id=1, source_target_pairs={{0,48},{8,56},{16,0},{24,8},{32,16},{40,24},{48,32},{56,40},{1,49}... | collective-permute-start | bytes 491528 | tf_op jit(solution)/shard_map/ppermute | solution.py:360
  110.4 7.6 %collective-permute-done.16.refs_3_ = bf16[128,640]{1,0:T(8,128)(2,1)S(1)} collective-permute-done((bf16[128,640]{1,0:T(8,128)(2,1)}, bf16[128,640]{1,0:T(8,128)(2,1)S(1)}, u32[]{:S(2)}, u32[]{:S(2)}) %collective-permute-start.16) | collective-permute-done | bytes 163872 | tf_op jit(solution)/shard_map/ppermute | solution.py:360
  127.2 5.9 %collective-permute-done.17.refs_4_ = bf16[128,640]{1,0:T(8,128)(2,1)S(1)} collective-permute-done((bf16[128,640]{1,0:T(8,128)(2,1)S(1)}, bf16[128,640]{1,0:T(8,128)(2,1)S(1)}, u32[]{:S(2)}, u32[]{:S(2)}) %collective-permute-start.17) | collective-permute-done | bytes 163872 | tf_op jit(solution)/shard_map/ppermute | solution.py:360
  133.1 9.5 %collective-permute-done.18.refs_5_ = bf16[128,640]{1,0:T(8,128)(2,1)S(1)} collective-permute-done((bf16[128,640]{1,0:T(8,128)(2,1)S(1)}, bf16[128,640]{1,0:T(8,128)(2,1)S(1)}, u32[]{:S(2)}, u32[]{:S(2)}) %collective-permute-start.18) | collective-permute-done | bytes 163872 | tf_op jit(solution)/shard_map/ppermute | solution.py:360
  143.9 4.1 %route.1 = (bf16[128,640]{1,0:T(8,128)(2,1)}, bf16[128,640]{1,0:T(8,128)(2,1)}, bf16[128,640]{1,0:T(8,128)(2,1)}, bf16[128,640]{1,0:T(8,128)(2,1)}, bf16[128,640...) custom-call(s32[1024,1]{1,0:T(8,128)} %reshape.182.refs_0_, ...), custom_call_target="tpu_custom_call" | custom-call | flops 13200000000 | bytes 1048576 | tf_op jit(solution)/shard_map/route/pallas_call | solution.py:187
  153.0 2.3 %collective-permute-start.25 = (bf16[128,640]{1,0:T(8,128)(2,1)}, bf16[128,640]{1,0:T(8,128)(2,1)S(1)}, u32[]{:S(2)}, u32[]{:S(2)}) collective-permute-start(bf16[128,640]{1,0:T(8,128)(2,1)} %get-tuple-element.29), channel_id=1, source_target_pairs={{0,128},{4,132},{64,192},{68,196},{128,0},{132,4},{192,64},{196,68... | collective-permute-start | bytes 491528 | tf_op jit(solution)/shard_map/ppermute | solution.py:375
  161.3 3.1 %collective-permute-done.25.refs_3_.refs_4_ = bf16[128,640]{1,0:T(8,128)(2,1)S(1)} collective-permute-done((bf16[128,640]{1,0:T(8,128)(2,1)}, bf16[128,640]{1,0:T(8,128)(2,1)S(1)}, u32[]{:S(2)}, u32[]{:S(2)}) %collective-permute-start.25) | collective-permute-done | bytes 163872 | tf_op jit(solution)/shard_map/ppermute | solution.py:375
  164.4 3.7 %collective-permute-done.26.refs_4_.refs_5_ = bf16[128,640]{1,0:T(8,128)(2,1)S(1)} collective-permute-done((bf16[128,640]{1,0:T(8,128)(2,1)}, bf16[128,640]{1,0:T(8,128)(2,1)S(1)}, u32[]{:S(2)}, u32[]{:S(2)}) %collective-permute-start.26) | collective-permute-done | bytes 163872 | tf_op jit(solution)/shard_map/ppermute | solution.py:375
  170.5 6.8 %output_map.1 = (bf16[128,1024]{1,0:T(8,128)(2,1)}, bf16[128,1024]{1,0:T(8,128)(2,1)}, bf16[128,1024]{1,0:T(8,128)(2,1)}, bf16[128,1024]{1,0:T(8,128)(2,1)}) custom-call(s32[2]{0:T(128)} %copy-done.4, bf16[128,640]{1,0:T(8,128)(2,1)} %get-tuple-element.37.refs_0_, bf16[128,640]{1,0:T(8,128)(2,1)} %copy-done.24, bf16[128,640]{1,0:T(8,128)(2,1)} %copy-done.25, ...), custom_call_target="tpu_custom_call" | custom-call | flops 19800000512 | bytes 1048576 | tf_op jit(solution)/shard_map/output_map/pallas_call | solution.py:218
  178.4 2.4 %collective-permute-start.33 = (bf16[128,1024]{1,0:T(8,128)(2,1)}, bf16[128,1024]{1,0:T(8,128)(2,1)S(1)}, u32[]{:S(2)}, u32[]{:S(2)}) collective-permute-start(bf16[128,1024]{1,0:T(8,128)(2,1)} %get-tuple-element.40), channel_id=1, source_target_pairs={{0,2},{1,3},{2,0},{3,1},{4,6},{5,7},{6,4},{7,5},{8,10},{9,11},{10,... | collective-permute-start | bytes 786440 | tf_op jit(solution)/shard_map/ppermute | solution.py:360
  181.1 3.4 %spread.1 = (bf16[8,32,640]{2,1,0:T(8,128)(2,1)}, bf16[8,32,640]{2,1,0:T(8,128)(2,1)}, bf16[8,32,640]{2,1,0:T(8,128)(2,1)}, bf16[8,32,640]{2,1,0:T(8,128)(2,1)}) custom-call(s32[32]{0:T(128)} %compare_select_fusion.6.source, bf16[16,512,640]{2,1,0:T(8,128)(2,1)} %bitcast.31, bf16[128,640]{1,0:T(8,128)(2,1)} %copy-done.24, bf16[128,640]{1,0:T(8,128)(2,1)} %copy-done.25, ...), custom_call_target="tpu_custom_call" | custom-call | flops 13200000000 | bytes 1048576 | tf_op jit(solution)/shard_map/spread/pallas_call | solution.py:322
  184.5 2.2 %collective-permute-start.29 = (bf16[8,32,640]{2,1,0:T(8,128)(2,1)}, bf16[8,32,640]{2,1,0:T(8,128)(2,1)S(1)}, u32[]{:S(2)}, u32[]{:S(2)}) collective-permute-start(bf16[8,32,640]{2,1,0:T(8,128)(2,1)} %get-tuple-element.34), channel_id=1, source_target_pairs={{0,64},{64,128},{128,192},{192,0},{1,65},{65,129},{129,193},{193,1... | collective-permute-start | bytes 983048 | tf_op jit(solution)/shard_map/ppermute | solution.py:360
  189.3 3.9 %collective-permute-done.33.p2 = bf16[128,1024]{1,0:T(8,128)(2,1)S(1)} collective-permute-done((bf16[128,1024]{1,0:T(8,128)(2,1)}, bf16[128,1024]{1,0:T(8,128)(2,1)S(1)}, u32[]{:S(2)}, u32[]{:S(2)}) %collective-permute-start.33) | collective-permute-done | bytes 262176 | tf_op jit(solution)/shard_map/ppermute | solution.py:360
  194.0 2.3 %place.1 = bf16[160,1024]{1,0:T(8,128)(2,1)} custom-call(bf16[128,1024]{1,0:T(8,128)(2,1)} %get-tuple-element.38.p0, bf16[128,1024]{1,0:T(8,128)(2,1)} %copy-done.21, bf16[128,1024]{1,0:T(8,128)(2,1)} %copy-done.22, bf16[128,1024]{1,0:T(8,128)(2,1)} %copy-done.23, f32[1,1024]{1,0:T(1,128)} %bitcast.34, s32[160,1]{1,0:T(8,128)} %copy.43.source), custom_call_target="tpu_custom_call" | custom-call | flops 9900000256 | bytes 1048576 | tf_op jit(solution)/shard_map/place/pallas_call | solution.py:249
  196.3 5.9 %collective-permute-done.30.refs_2_ = bf16[8,32,640]{2,1,0:T(8,128)(2,1)S(1)} collective-permute-done((bf16[8,32,640]{2,1,0:T(8,128)(2,1)}, bf16[8,32,640]{2,1,0:T(8,128)(2,1)S(1)}, u32[]{:S(2)}, u32[]{:S(2)}) %collective-permute-start.30) | collective-permute-done | bytes 327712 | tf_op jit(solution)/shard_map/ppermute | solution.py:360
  203.2 2.2 %unpack.1 = bf16[320,512]{1,0:T(8,128)(2,1)} custom-call(bf16[8,32,640]{2,1,0:T(8,128)(2,1)} %get-tuple-element.33.refs_0_, bf16[8,32,640]{2,1,0:T(8,128)(2,1)} %copy-done.15, bf16[8,32,640]{2,1,0:T(8,128)(2,1)} %copy-done.16, bf16[8,32,640]{2,1,0:T(8,128)(2,1)} %copy-done.19), custom_call_target="tpu_custom_call" | custom-call | flops 6600000000 | bytes 1048576 | tf_op jit(solution)/shard_map/unpack/pallas_call | solution.py:350
  (175 shorter events, 56.2 us)
Async XLA Ops:
  7.2 85.6 %all-gather.7.cloned.1.call-start = ((), (), s32[]{:S(2)}) async-start(), calls=%async_computation.1 | async-start | bytes 6963200 | tf_op jit(solution)/shard_map/all_gather | solution.py:422
  19.6 150.2 %all-gather.5.cloned.1.call-start = ((), (), s32[]{:S(2)}) async-start(), calls=%async_computation | async-start | bytes 11141120 | tf_op jit(solution)/shard_map/all_gather | solution.py:422
  19.7 8.4 %collective-permute-start = (bf16[320,512]{1,0:T(8,128)(2,1)S(1)}, bf16[320,512]{1,0:T(8,128)(2,1)S(1)}, u32[]{:S(2)}, u32[]{:S(2)}) collective-permute-start(bf16[320,512]{1,0:T(8,128)(2,1)S(1)} %bitcast.23), channel_id=1, source_target_pairs={{0,1},{1,2},{2,3},{3,0},{4,5},{5,6},{6,7},{7,4},{8,9},{9,10},{10,1... | collective-permute-start | bytes 983048 | tf_op jit(solution)/shard_map/ppermute | solution.py:360
  21.0 15.4 %collective-permute-start.1 = (bf16[320,512]{1,0:T(8,128)(2,1)S(1)}, bf16[320,512]{1,0:T(8,128)(2,1)S(1)}, u32[]{:S(2)}, u32[]{:S(2)}) collective-permute-start(bf16[320,512]{1,0:T(8,128)(2,1)S(1)} %bitcast.24), channel_id=1, source_target_pairs={{0,2},{1,3},{2,0},{3,1},{4,6},{5,7},{6,4},{7,5},{8,10},{9,11},{10,... | collective-permute-start | bytes 983048 | tf_op jit(solution)/shard_map/ppermute | solution.py:360
  23.4 13.5 %collective-permute-start.2 = (bf16[320,512]{1,0:T(8,128)(2,1)S(1)}, bf16[320,512]{1,0:T(8,128)(2,1)}, u32[]{:S(2)}, u32[]{:S(2)}) collective-permute-start(bf16[320,512]{1,0:T(8,128)(2,1)S(1)} %bitcast.25), channel_id=1, source_target_pairs={{0,3},{1,0},{2,1},{3,2},{4,7},{5,4},{6,5},{7,6},{8,11},{9,8},{10,9... | collective-permute-start | bytes 983048 | tf_op jit(solution)/shard_map/ppermute | solution.py:360
  48.9 10.3 %collective-permute-start.3 = (bf16[320,512]{1,0:T(8,128)(2,1)}, bf16[320,512]{1,0:T(8,128)(2,1)S(1)}, u32[]{:S(2)}, u32[]{:S(2)}) collective-permute-start(bf16[320,512]{1,0:T(8,128)(2,1)} %get-tuple-element.23), channel_id=1, source_target_pairs={{0,1},{1,2},{2,3},{3,0},{4,5},{5,6},{6,7},{7,4},{8,9},{9,10},{10,1... | collective-permute-start | bytes 983048 | tf_op jit(solution)/shard_map/ppermute | solution.py:360
  51.0 16.9 %collective-permute-start.4 = (bf16[320,512]{1,0:T(8,128)(2,1)}, bf16[320,512]{1,0:T(8,128)(2,1)S(1)}, u32[]{:S(2)}, u32[]{:S(2)}) collective-permute-start(bf16[320,512]{1,0:T(8,128)(2,1)} %get-tuple-element.24), channel_id=1, source_target_pairs={{0,2},{1,3},{2,0},{3,1},{4,6},{5,7},{6,4},{7,5},{8,10},{9,11},{10,... | collective-permute-start | bytes 983048 | tf_op jit(solution)/shard_map/ppermute | solution.py:360
  53.6 14.3 %collective-permute-start.5 = (bf16[320,512]{1,0:T(8,128)(2,1)}, bf16[320,512]{1,0:T(8,128)(2,1)S(1)}, u32[]{:S(2)}, u32[]{:S(2)}) collective-permute-start(bf16[320,512]{1,0:T(8,128)(2,1)} %get-tuple-element.25), channel_id=1, source_target_pairs={{0,3},{1,0},{2,1},{3,2},{4,7},{5,4},{6,5},{7,6},{8,11},{9,8},{10,9... | collective-permute-start | bytes 983048 | tf_op jit(solution)/shard_map/ppermute | solution.py:360
  56.1 12.8 %collective-permute-start.6 = (bf16[64,640]{1,0:T(8,128)(2,1)}, bf16[64,640]{1,0:T(8,128)(2,1)S(1)}, u32[]{:S(2)}, u32[]{:S(2)}) collective-permute-start(bf16[64,640]{1,0:T(8,128)(2,1)} %hold.1.refs_0_), channel_id=1, source_target_pairs={{0,64},{64,128},{128,192},{192,0},{1,65},{65,129},{129,193},{193,1... | collective-permute-start | bytes 245768 | tf_op jit(solution)/shard_map/ppermute | solution.py:360
  56.1 12.8 %collective-permute-start.7 = (bf16[64,640]{1,0:T(8,128)(2,1)}, bf16[64,640]{1,0:T(8,128)(2,1)S(1)}, u32[]{:S(2)}, u32[]{:S(2)}) collective-permute-start(bf16[64,640]{1,0:T(8,128)(2,1)} %hold.1.refs_0_), channel_id=1, source_target_pairs={{0,128},{64,192},{128,0},{192,64},{1,129},{65,193},{129,1},{193,65... | collective-permute-start | bytes 245768 | tf_op jit(solution)/shard_map/ppermute | solution.py:360
  59.2 9.7 %collective-permute-start.8 = (bf16[64,640]{1,0:T(8,128)(2,1)}, bf16[64,640]{1,0:T(8,128)(2,1)S(1)}, u32[]{:S(2)}, u32[]{:S(2)}) collective-permute-start(bf16[64,640]{1,0:T(8,128)(2,1)} %hold.1.refs_0_), channel_id=1, source_target_pairs={{0,192},{64,0},{128,64},{192,128},{1,193},{65,1},{129,65},{193,129... | collective-permute-start | bytes 245768 | tf_op jit(solution)/shard_map/ppermute | solution.py:360
  74.5 9.2 %collective-permute-start.10 = (bf16[320,512]{1,0:T(8,128)(2,1)S(1)}, bf16[320,512]{1,0:T(8,128)(2,1)S(1)}, u32[]{:S(2)}, u32[]{:S(2)}) collective-permute-start(bf16[320,512]{1,0:T(8,128)(2,1)S(1)} %copy-done.6), channel_id=1, source_target_pairs={{0,2},{1,3},{2,0},{3,1},{4,6},{5,7},{6,4},{7,5},{8,10},{9,11},{10,... | collective-permute-start | bytes 983048 | tf_op jit(solution)/shard_map/ppermute | solution.py:360
  75.8 17.0 %collective-permute-start.11 = (bf16[320,512]{1,0:T(8,128)(2,1)S(1)}, bf16[320,512]{1,0:T(8,128)(2,1)S(1)}, u32[]{:S(2)}, u32[]{:S(2)}) collective-permute-start(bf16[320,512]{1,0:T(8,128)(2,1)S(1)} %copy-done.6), channel_id=1, source_target_pairs={{0,3},{1,0},{2,1},{3,2},{4,7},{5,4},{6,5},{7,6},{8,11},{9,8},{10,9... | collective-permute-start | bytes 983048 | tf_op jit(solution)/shard_map/ppermute | solution.py:360
  78.5 14.3 %collective-permute-start.9 = (bf16[320,512]{1,0:T(8,128)(2,1)S(1)}, bf16[320,512]{1,0:T(8,128)(2,1)S(1)}, u32[]{:S(2)}, u32[]{:S(2)}) collective-permute-start(bf16[320,512]{1,0:T(8,128)(2,1)S(1)} %copy-done.6), channel_id=1, source_target_pairs={{0,1},{1,2},{2,3},{3,0},{4,5},{5,6},{6,7},{7,4},{8,9},{9,10},{10,1... | collective-permute-start | bytes 983048 | tf_op jit(solution)/shard_map/ppermute | solution.py:360
  101.5 16.5 %collective-permute-start.16 = (bf16[128,640]{1,0:T(8,128)(2,1)}, bf16[128,640]{1,0:T(8,128)(2,1)S(1)}, u32[]{:S(2)}, u32[]{:S(2)}) collective-permute-start(bf16[128,640]{1,0:T(8,128)(2,1)} %expand.1.refs_1_), channel_id=1, source_target_pairs={{0,16},{8,24},{16,32},{24,40},{32,48},{40,56},{48,0},{56,8},{1,17}... | collective-permute-start | bytes 491528 | tf_op jit(solution)/shard_map/ppermute | solution.py:360
  104.7 15.6 %collective-permute-start.19 = (bf16[128,640]{1,0:T(8,128)(2,1)}, bf16[128,640]{1,0:T(8,128)(2,1)S(1)}, u32[]{:S(2)}, u32[]{:S(2)}) collective-permute-start(bf16[128,640]{1,0:T(8,128)(2,1)} %expand.1.refs_1_), channel_id=1, source_target_pairs={{0,48},{8,56},{16,0},{24,8},{32,16},{40,24},{48,32},{56,40},{1,49}... | collective-permute-start | bytes 491528 | tf_op jit(solution)/shard_map/ppermute | solution.py:360
  107.8 18.3 %collective-permute-start.15 = (bf16[128,640]{1,0:T(8,128)(2,1)}, bf16[128,640]{1,0:T(8,128)(2,1)S(1)}, u32[]{:S(2)}, u32[]{:S(2)}) collective-permute-start(bf16[128,640]{1,0:T(8,128)(2,1)} %expand.1.refs_1_), channel_id=1, source_target_pairs={{0,8},{8,16},{16,24},{24,32},{32,40},{40,48},{48,56},{56,0},{1,9},... | collective-permute-start | bytes 491528 | tf_op jit(solution)/shard_map/ppermute | solution.py:360
  108.5 18.6 %collective-permute-start.21 = (bf16[128,640]{1,0:T(8,128)(2,1)}, bf16[128,640]{1,0:T(8,128)(2,1)S(1)}, u32[]{:S(2)}, u32[]{:S(2)}) collective-permute-start(bf16[128,640]{1,0:T(8,128)(2,1)} %expand.1.refs_1_), channel_id=1, source_target_pairs={{0,56},{8,0},{16,8},{24,16},{32,24},{40,32},{48,40},{56,48},{1,57}... | collective-permute-start | bytes 491528 | tf_op jit(solution)/shard_map/ppermute | solution.py:360
  118.0 15.1 %collective-permute-start.17 = (bf16[128,640]{1,0:T(8,128)(2,1)S(1)}, bf16[128,640]{1,0:T(8,128)(2,1)S(1)}, u32[]{:S(2)}, u32[]{:S(2)}) collective-permute-start(bf16[128,640]{1,0:T(8,128)(2,1)S(1)} %collective-permute-done.16.refs_3_), channel_id=1, source_target_pairs={{0,8},{8,16},{16,24},{24,32},{32,40},{40,48},{48,56},{56,0},{1,9},... | collective-permute-start | bytes 491528 | tf_op jit(solution)/shard_map/ppermute | solution.py:360
  119.9 22.7 %collective-permute-start.18 = (bf16[128,640]{1,0:T(8,128)(2,1)S(1)}, bf16[128,640]{1,0:T(8,128)(2,1)S(1)}, u32[]{:S(2)}, u32[]{:S(2)}) collective-permute-start(bf16[128,640]{1,0:T(8,128)(2,1)S(1)} %collective-permute-done.16.refs_3_), channel_id=1, source_target_pairs={{0,16},{8,24},{16,32},{24,40},{32,48},{40,56},{48,0},{56,8},{1,17}... | collective-permute-start | bytes 491528 | tf_op jit(solution)/shard_map/ppermute | solution.py:360
  120.3 22.3 %collective-permute-start.20 = (bf16[128,640]{1,0:T(8,128)(2,1)S(1)}, bf16[128,640]{1,0:T(8,128)(2,1)S(1)}, u32[]{:S(2)}, u32[]{:S(2)}) collective-permute-start(bf16[128,640]{1,0:T(8,128)(2,1)S(1)} %collective-permute-done.19.refs_7_), channel_id=1, source_target_pairs={{0,56},{8,0},{16,8},{24,16},{32,24},{40,32},{48,40},{56,48},{1,57}... | collective-permute-start | bytes 491528 | tf_op jit(solution)/shard_map/ppermute | solution.py:360
  151.1 10.2 %collective-permute-start.24 = (bf16[128,640]{1,0:T(8,128)(2,1)}, bf16[128,640]{1,0:T(8,128)(2,1)S(1)}, u32[]{:S(2)}, u32[]{:S(2)}) collective-permute-start(bf16[128,640]{1,0:T(8,128)(2,1)} %get-tuple-element.28), channel_id=1, source_target_pairs={{0,68},{4,64},{64,132},{68,128},{128,196},{132,192},{192,4},{196,0... | collective-permute-start | bytes 491528 | tf_op jit(solution)/shard_map/ppermute | solution.py:375
  153.0 11.4 %collective-permute-start.25 = (bf16[128,640]{1,0:T(8,128)(2,1)}, bf16[128,640]{1,0:T(8,128)(2,1)S(1)}, u32[]{:S(2)}, u32[]{:S(2)}) collective-permute-start(bf16[128,640]{1,0:T(8,128)(2,1)} %get-tuple-element.29), channel_id=1, source_target_pairs={{0,128},{4,132},{64,192},{68,196},{128,0},{132,4},{192,64},{196,68... | collective-permute-start | bytes 491528 | tf_op jit(solution)/shard_map/ppermute | solution.py:375
  155.3 12.8 %collective-permute-start.26 = (bf16[128,640]{1,0:T(8,128)(2,1)}, bf16[128,640]{1,0:T(8,128)(2,1)S(1)}, u32[]{:S(2)}, u32[]{:S(2)}) collective-permute-start(bf16[128,640]{1,0:T(8,128)(2,1)} %get-tuple-element.30), channel_id=1, source_target_pairs={{0,132},{4,128},{64,196},{68,192},{128,4},{132,0},{192,68},{196,64... | collective-permute-start | bytes 491528 | tf_op jit(solution)/shard_map/ppermute | solution.py:375
  156.3 11.8 %collective-permute-start.27 = (bf16[128,640]{1,0:T(8,128)(2,1)}, bf16[128,640]{1,0:T(8,128)(2,1)S(1)}, u32[]{:S(2)}, u32[]{:S(2)}) collective-permute-start(bf16[128,640]{1,0:T(8,128)(2,1)} %get-tuple-element.31), channel_id=1, source_target_pairs={{0,192},{4,196},{64,0},{68,4},{128,64},{132,68},{192,128},{196,132... | collective-permute-start | bytes 491528 | tf_op jit(solution)/shard_map/ppermute | solution.py:375
  157.5 12.3 %collective-permute-start.28 = (bf16[128,640]{1,0:T(8,128)(2,1)}, bf16[128,640]{1,0:T(8,128)(2,1)S(1)}, u32[]{:S(2)}, u32[]{:S(2)}) collective-permute-start(bf16[128,640]{1,0:T(8,128)(2,1)} %get-tuple-element.32), channel_id=1, source_target_pairs={{0,196},{4,192},{64,4},{68,0},{128,68},{132,64},{192,132},{196,128... | collective-permute-start | bytes 491528 | tf_op jit(solution)/shard_map/ppermute | solution.py:375
  177.2 11.2 %collective-permute-start.32 = (bf16[128,1024]{1,0:T(8,128)(2,1)}, bf16[128,1024]{1,0:T(8,128)(2,1)S(1)}, u32[]{:S(2)}, u32[]{:S(2)}) collective-permute-start(bf16[128,1024]{1,0:T(8,128)(2,1)} %get-tuple-element.39), channel_id=1, source_target_pairs={{0,1},{1,2},{2,3},{3,0},{4,5},{5,6},{6,7},{7,4},{8,9},{9,10},{10,1... | collective-permute-start | bytes 786440 | tf_op jit(solution)/shard_map/ppermute | solution.py:360
  178.4 14.8 %collective-permute-start.33 = (bf16[128,1024]{1,0:T(8,128)(2,1)}, bf16[128,1024]{1,0:T(8,128)(2,1)S(1)}, u32[]{:S(2)}, u32[]{:S(2)}) collective-permute-start(bf16[128,1024]{1,0:T(8,128)(2,1)} %get-tuple-element.40), channel_id=1, source_target_pairs={{0,2},{1,3},{2,0},{3,1},{4,6},{5,7},{6,4},{7,5},{8,10},{9,11},{10,... | collective-permute-start | bytes 786440 | tf_op jit(solution)/shard_map/ppermute | solution.py:360
  180.8 12.4 %collective-permute-start.34 = (bf16[128,1024]{1,0:T(8,128)(2,1)}, bf16[128,1024]{1,0:T(8,128)(2,1)S(1)}, u32[]{:S(2)}, u32[]{:S(2)}) collective-permute-start(bf16[128,1024]{1,0:T(8,128)(2,1)} %get-tuple-element.41), channel_id=1, source_target_pairs={{0,3},{1,0},{2,1},{3,2},{4,7},{5,4},{6,5},{7,6},{8,11},{9,8},{10,9... | collective-permute-start | bytes 786440 | tf_op jit(solution)/shard_map/ppermute | solution.py:360
  184.5 11.7 %collective-permute-start.29 = (bf16[8,32,640]{2,1,0:T(8,128)(2,1)}, bf16[8,32,640]{2,1,0:T(8,128)(2,1)S(1)}, u32[]{:S(2)}, u32[]{:S(2)}) collective-permute-start(bf16[8,32,640]{2,1,0:T(8,128)(2,1)} %get-tuple-element.34), channel_id=1, source_target_pairs={{0,64},{64,128},{128,192},{192,0},{1,65},{65,129},{129,193},{193,1... | collective-permute-start | bytes 983048 | tf_op jit(solution)/shard_map/ppermute | solution.py:360
  186.8 15.4 %collective-permute-start.30 = (bf16[8,32,640]{2,1,0:T(8,128)(2,1)}, bf16[8,32,640]{2,1,0:T(8,128)(2,1)S(1)}, u32[]{:S(2)}, u32[]{:S(2)}) collective-permute-start(bf16[8,32,640]{2,1,0:T(8,128)(2,1)} %get-tuple-element.35), channel_id=1, source_target_pairs={{0,128},{64,192},{128,0},{192,64},{1,129},{65,193},{129,1},{193,65... | collective-permute-start | bytes 983048 | tf_op jit(solution)/shard_map/ppermute | solution.py:360
  188.4 14.0 %collective-permute-start.31 = (bf16[8,32,640]{2,1,0:T(8,128)(2,1)}, bf16[8,32,640]{2,1,0:T(8,128)(2,1)S(1)}, u32[]{:S(2)}, u32[]{:S(2)}) collective-permute-start(bf16[8,32,640]{2,1,0:T(8,128)(2,1)} %get-tuple-element.36), channel_id=1, source_target_pairs={{0,192},{64,0},{128,64},{192,128},{1,193},{65,1},{129,65},{193,129... | collective-permute-start | bytes 983048 | tf_op jit(solution)/shard_map/ppermute | solution.py:360
  (49 other events, 389.2 us)
Sparse Core Ops, SparseCore 0:
  19.8 50.5 all-gather.6
  72.4 89.1 all-gather.4
